TPU v7x, 128 devices: a whole 4x4x4 slice. The times are simulated.
128 devices in a mesh: wide: 16 (over y, x), narrow: 8 (over z, core).
Axes of the slice: x: 4, y: 4, z: 4, core: 2. Of those that a mesh axis runs over, the one named last changes fastest.
Arguments:
- features: bfloat16 [131072, 1024], P(('wide', 'narrow')), may hold values from -6 to 6
- cluster_ids: int32 [131072, 1], P(('wide', 'narrow')), may hold values from 0 to 511; in each aligned block of 8192 rows (0 to 8191, 8192 to 16383, ...) at most 32 rows name the same one
- cluster_slots: int32 [512], replicated, may hold values from 0 to 511, each once
- w_first: bfloat16 [1024, 1024], replicated, may hold values from -0.1875 to 0.1875
- w_second: bfloat16 [1024, 1024], replicated, may hold values from -0.1875 to 0.1875
- w_third: bfloat16 [1024, 1024], replicated, may hold values from -0.1875 to 0.1875
- emb_gain: float32 [1024], replicated, may hold values from 0.25 to 1.75
- queries: bfloat16 [64, 1024], P('wide', 'narrow'), may hold values from -0.1875 to 0.1875
Outputs:
- best_scores: float32 [64, 512], P('narrow', 'wide')
- index_slab: bfloat16 [16, 512, 32, 1024], P(None, 'wide', None, 'narrow')
Inputs may be any that keep to these rules, and one draw needn't show every extreme that they name: `cluster_ids`: every cluster is named by some item. In each aligned block of 8 * 1024 rows no cluster is named by more than 32 rows, a bound that some block reaches. `cluster_slots`: each number once. Output columns k * 32 to (k + 1) * 32 - 1 belong to the clusters owned by index k of wide.
All inputs are finite; a program needn't handle non-finite values.
Results may differ from a plain program's by a relative error of at most 0.014.
Values may be sent and summed in bfloat16 or wider, within the bound.
A program may use at most 192 MiB of HBM per device.

v0:
```python
import math

import jax
import jax.numpy as jnp
from jax import lax
from jax.sharding import PartitionSpec as P

CL_DEV = 32


def slot_table(id_list, cluster_slots, total):
    levels = jnp.arange(total, dtype=jnp.int32)
    onehot = (id_list[:, None] == levels[None, :]).astype(jnp.bfloat16)
    high_part = (cluster_slots // 64).astype(jnp.bfloat16)
    low_part = (cluster_slots % 64).astype(jnp.bfloat16)
    slot_value = 64.0 * jnp.dot(onehot, high_part, preferred_element_type=jnp.float32) + jnp.dot(
        onehot, low_part, preferred_element_type=jnp.float32
    )
    return (onehot, slot_value.astype(jnp.int32))


def cluster_ranks(onehot):
    count, total = onehot.shape
    block = math.gcd(count, 256)
    number = count // block
    stacked = onehot.reshape(number, block, total)
    inner = jnp.arange(block, dtype=jnp.int32)
    lower = (inner[:, None] >= inner[None, :]).astype(jnp.bfloat16)
    inside = jnp.einsum("rs,bsc->brc", lower, stacked, preferred_element_type=jnp.float32)
    block_sums = inside[:, -1, :]
    outer = jnp.arange(number, dtype=jnp.int32)
    before = (outer[:, None] > outer[None, :]).astype(jnp.float32)
    earlier = jnp.dot(
        before, block_sums, precision=lax.Precision.HIGHEST, preferred_element_type=jnp.float32
    )
    position = jnp.sum(stacked * (inside - 1.0 + earlier[:, None, :]), axis=2)
    return (position.reshape(count).astype(jnp.int32), jnp.sum(block_sums, axis=0))


def shards(features, cluster_ids, cluster_slots, w_first, w_second, w_third, emb_gain, queries):
    rows = features.shape[0]
    narrow_count = lax.axis_size("narrow")
    wide_count = lax.axis_size("wide")
    clusters_own = CL_DEV
    most_rows = 2 * narrow_count * rows // (wide_count * clusters_own)
    per_owner = clusters_own * most_rows
    total_clusters = cluster_slots.shape[0]
    slot_capacity = total_clusters * most_rows
    first = jax.nn.silu(jnp.dot(features, w_first, preferred_element_type=jnp.float32)).astype(
        jnp.bfloat16
    )
    second = jax.nn.silu(jnp.dot(first, w_second, preferred_element_type=jnp.float32)).astype(
        jnp.bfloat16
    )
    raw = jnp.dot(second, w_third, preferred_element_type=jnp.float32)
    scale = lax.rsqrt(jnp.mean(raw * raw, axis=1, keepdims=True) + 1e-06)
    embedding = (raw * scale * emb_gain).astype(jnp.bfloat16)
    width = embedding.shape[1]
    piece = width // narrow_count
    all_queries = lax.all_gather(queries, "wide", axis=0, tiled=True)
    own_queries = all_queries.shape[0] // narrow_count
    block_ids = lax.all_gather(cluster_ids[:, 0], "narrow", axis=0, tiled=True)
    block_rows = block_ids.shape[0]
    onehot, slot_of = slot_table(block_ids, cluster_slots, total_clusters)
    positions, per_cluster = cluster_ranks(onehot)
    flat_slot = slot_of * most_rows + positions
    slot_levels = jnp.arange(total_clusters, dtype=jnp.int32)
    matched = cluster_slots[:, None] == slot_levels[None, :]
    per_slot = jnp.sum(jnp.where(matched, per_cluster[:, None], 0.0), axis=0)
    slot_counts = per_slot.reshape(wide_count, clusters_own)
    sliced = lax.all_to_all(embedding, "narrow", split_axis=1, concat_axis=0, tiled=True)
    source = (
        jnp.full((slot_capacity,), block_rows, jnp.int32)
        .at[flat_slot]
        .set(jnp.arange(block_rows, dtype=jnp.int32))
    )
    padded = jnp.concatenate([sliced, jnp.zeros((1, piece), jnp.bfloat16)], axis=0)
    outgoing = jnp.take(padded, source, axis=0).reshape(wide_count, per_owner, piece)
    arrived, arrived_counts = (
        lax.all_to_all(outgoing, "wide", split_axis=0, concat_axis=0, tiled=True),
        lax.all_to_all(
            slot_counts.astype(jnp.bfloat16), "wide", split_axis=0, concat_axis=0, tiled=True
        ),
    )
    index_slab = arrived.reshape(wide_count, clusters_own, most_rows, piece)
    owned_items = arrived.reshape(wide_count * per_owner, piece)
    levels = jnp.arange(most_rows, dtype=jnp.float32)
    valid = levels[None, None, :] < arrived_counts.astype(jnp.float32)[:, :, None]
    scores = lax.psum_scatter(
        lax.dot_general(
            all_queries, owned_items, (((1,), (1,)), ((), ())), preferred_element_type=jnp.float32
        ).astype(jnp.bfloat16),
        "narrow",
        scatter_dimension=0,
        tiled=True,
    ).astype(jnp.float32)
    grouped = scores.reshape(own_queries, wide_count, clusters_own, most_rows)
    best = jnp.max(jnp.where(valid[None], grouped, -jnp.inf), axis=(1, 3))
    return (best, index_slab)


def solution(mesh):
    placed = (
        P(("wide", "narrow"), None),
        P(("wide", "narrow"), None),
        P(),
        P(),
        P(),
        P(),
        P(),
        P("wide", "narrow"),
    )
    return jax.shard_map(
        shards,
        mesh=mesh,
        in_specs=placed,
        out_specs=(P("narrow", "wide"), P(None, "wide", None, "narrow")),
        check_vma=False,
    )
```

profile of v0, /device:TPU:1, one launch (start us, length us, event | category | flops | bytes accessed | tf_op | source)
XLA Modules:
  0.0 323.1 jit_solution(1957439418634847948)
XLA Ops:
  7.2 6.7 %fusion.24 = f32[1024,1024]{1,0:T(8,128)} fusion(bf16[1024,1024]{1,0:T(8,128)(2,1)} %param.8, bf16[1024,1024]{1,0:T(8,128)(2,1)} %param.11), kind=kOutput, calls=%fused_computation.52 | convolution fusion | flops 2147483648 | bytes 8388608 | tf_op jit(solution)/shard_map/dot_general | solution.py:49
  13.9 9.8 %multiply_reduce_fusion.1 = (f32[1024]{0:T(1024)S(1)}, f32[1024,1024]{0,1:T(8,128)}) fusion(bf16[1024,1024]{1,0:T(8,128)(2,1)S(1)} %copy-done, bf16[1024,1024]{1,0:T(8,128)(2,1)} %param.12, f32[1024,1024]{1,0:T(8,128)} %fusion.24), kind=kOutput, calls=%fused_computation.16 | convolution fusion | flops 4307549184 | bytes 12587008 | tf_op jit(solution)/shard_map/dot_general | solution.py:55
  23.7 3.9 %multiply_convert_fusion = bf16[1024,1024]{0,1:T(8,128)(2,1)} fusion(f32[1024,1024]{0,1:T(8,128)} %get-tuple-element.7, f32[1024]{0:T(1024)S(1)} %copy-done.2, f32[1024]{0:T(1024)S(1)} %add_rsqrt_fusion), kind=kLoop, calls=%fused_computation.15 | loop fusion | flops 3145728 | bytes 6299648 | tf_op jit(solution)/shard_map/convert_element_type | solution.py:57
  27.6 6.8 %all-to-all-start.1 = ((bf16[1024,8,128]{0,2,1:T(8,128)(2,1)}), bf16[1024,8,128]{0,2,1:T(8,128)(2,1)}, u32[]{:S(2)}, u32[]{:S(2)}) async-start(bf16[1024,8,128]{0,2,1:T(8,128)(2,1)} %bitcast.35), calls=%async_computation.1 | async-start | bytes 4194304 | tf_op jit(solution)/shard_map/all_to_all | solution.py:71
  34.5 32.9 %all-gather = s32[8192,1]{0,1:T(1,128)S(1)} all-gather(s32[1024,1]{0,1:T(1,128)S(1)} %copy-done.3), channel_id=2, replica_groups=mesh['wide'=16,'narrow'=8] {'narrow'}, dimensions={0}, use_global_device_ids=true | all-gather | bytes 36864 | tf_op jit(solution)/shard_map/all_gather | solution.py:62
  67.4 0.5 broadcast.76
  67.9 0.7 reduce.4
  68.6 4.9 %fusion.5 = f32[32,256,512]{2,1,0:T(8,128)S(1)} fusion(s32[32,256]{1,0:T(8,128)S(1)} %eq.41), kind=kOutput, calls=%fused_computation.11 | convolution fusion | flops 2151743488 | bytes 16809984 | tf_op jit(solution)/shard_map/rs,bsc->brc/dot_general | solution.py:29
  73.8 4.8 %multiply_reduce_fusion = f32[32,256]{1,0:T(8,128)S(1)} fusion(f32[32,256,512]{2,1,0:T(8,128)S(1)} %fusion.5, f32[32,512]{1,0:T(8,128)S(1)} %fusion.13, s32[32,256]{1,0:T(8,128)S(1)} %eq.41), kind=kLoop, calls=%fused_computation.4 | loop fusion | flops 29351936 | bytes 16908288 | tf_op jit(solution)/shard_map/reduce_sum | solution.py:36
  78.7 3.6 %fusion.2 = f32[1,8192]{1,0:T(1,128)S(1)} fusion(bf16[512,1]{0,1:T(2,128)(2,1)S(1)} %reshape.116, s32[8192]{0:T(1024)S(1)} %bitcast.37), kind=kOutput, calls=%fused_computation.7 | convolution fusion | flops 12582912 | bytes 66560 | tf_op jit(solution)/shard_map/dot_general | solution.py:16
  82.3 3.6 %fusion.1 = f32[1,8192]{1,0:T(1,128)S(1)} fusion(bf16[512,1]{0,1:T(2,128)(2,1)S(1)} %reshape.118, s32[8192]{0:T(1024)S(1)} %bitcast.38), kind=kOutput, calls=%fused_computation.6 | convolution fusion | flops 12582912 | bytes 66560 | tf_op jit(solution)/shard_map/dot_general | solution.py:16
  85.9 30.5 %scatter_custom_fusion = s32[16384]{0:T(1024)S(1)} fusion(s32[8192]{0:T(1024)S(1)} %compare_select_fusion.1, s32[8192]{0:T(1024)S(1)} %iota.36, s32[]{:T(128)} %constant.51.clone.1), kind=kCustom, calls=%fused_computation.36 | custom fusion | bytes 65540 | tf_op jit(solution)/shard_map/scatter | solution.py:75
  116.5 3.9 %copy.15 = bf16[8,1024,128]{2,1,0:T(8,128)(2,1)} copy(bf16[8,1024,128]{1,2,0:T(8,128)(2,1)} %bitcast.7) | data formatting | bytes 4194304 | tf_op jit(solution)/shard_map/all_to_all | solution.py:71
  120.4 2.7 concatenate.3
  123.1 57.4 %gather_fusion = bf16[16384,128]{1,0:T(8,128)(2,1)} fusion(bf16[8193,128]{1,0:T(8,128)(2,1)} %concatenate.3, s32[16384]{0:T(1024)S(1)} %fusion.16), kind=kCustom, calls=%fused_computation | custom fusion | bytes 8454144 | tf_op jit(solution)/shard_map/jit(_take)/gather | solution.py:78
  180.5 7.6 %broadcast_select_fusion = bf16[16,1024,128]{2,1,0:T(8,128)(2,1)} fusion(bf16[16,1024,128]{2,1,0:T(8,128)(2,1)} %bitcast.34, pred[16,1024]{1,0:T(8,128)(4,1)S(1)} %broadcast_in_dim.65), kind=kLoop, calls=%fused_computation.19 | loop fusion | flops 2097152 | bytes 8404992 | tf_op jit(solution)/shard_map/jit(_take)/select_n | solution.py:78
  188.1 6.9 %all-to-all-start.2 = ((bf16[16,1024,128]{2,1,0:T(8,128)(2,1)}), bf16[16,1024,128]{2,1,0:T(8,128)(2,1)}, u32[]{:S(2)}, u32[]{:S(2)}) async-start(bf16[16,1024,128]{2,1,0:T(8,128)(2,1)} %broadcast_select_fusion), calls=%async_computation.2 | async-start | bytes 8388608 | tf_op jit(solution)/shard_map/all_to_all | solution.py:80
  195.1 72.3 %all-gather.1 = bf16[16,4,128]{2,1,0:T(4,128)(2,1)S(1)} all-gather(bf16[1,4,128]{2,1,0:T(4,128)(2,1)S(1)} %bitcast.44), channel_id=1, replica_groups=mesh['wide'=16,'narrow'=8] {'wide'}, dimensions={0}, use_global_device_ids=true | all-gather | bytes 17408 | tf_op jit(solution)/shard_map/all_gather | solution.py:60
  267.4 5.1 %fusion = bf16[64,16384]{1,0:T(8,128)(2,1)} fusion(bf16[16384,128]{1,0:T(8,128)(2,1)} %bitcast.10, bf16[64,128]{1,0:T(8,128)(2,1)S(1)} %bitcast.40), kind=kOutput, calls=%fused_computation.3 | convolution fusion | flops 269484032 | bytes 6307840 | tf_op jit(solution)/shard_map/dot_general | solution.py:90
  272.8 10.8 %all_to_all.30 = bf16[16,1,32]{2,1,0:T(2,128)(2,1)S(1)} all-to-all(bf16[16,1,32]{2,1,0:T(2,128)(2,1)S(1)} %convert_element_type.80), channel_id=1, replica_groups=mesh['wide'=16,'narrow'=8] {'wide'}, dimensions={0} | all-to-all | bytes 2048 | tf_op jit(solution)/shard_map/all_to_all | solution.py:81
  283.7 21.9 %reduce-scatter.2.cloned.1.call-done = bf16[8,16384]{1,0:T(8,128)(2,1)} async-done(((bf16[64,16384]{1,0:T(8,128)(2,1)}), bf16[8,16384]{1,0:T(8,128)(2,1)}) %reduce-scatter.2.cloned.1.call-update) | async-done | bytes 262160 | tf_op jit(solution)/shard_map/reduce_scatter | solution.py:89
  305.7 3.0 reshape.92
  308.6 2.5 select_reduce_fusion
  311.2 5.1 %copy.23 = bf16[16,32,32,128]{3,2,1,0:T(8,128)(2,1)} copy(bf16[16,32,32,128]{3,2,1,0:T(8,128)(2,1)} %bitcast.14) | data formatting | bytes 8388608
  (32 shorter events, 1.0 us)
Async XLA Ops:
  7.2 6.7 %copy-start = (bf16[1024,1024]{1,0:T(8,128)(2,1)S(1)}, bf16[1024,1024]{1,0:T(8,128)(2,1)}, u32[]{:S(2)}) copy-start(bf16[1024,1024]{1,0:T(8,128)(2,1)} %param.13) | copy-start | bytes 6291460
  13.9 9.8 %copy-start.2 = (f32[1024]{0:T(1024)S(1)}, f32[1024]{0:T(1024)}, u32[]{:S(2)}) copy-start(f32[1024]{0:T(1024)} %param.14) | copy-start | bytes 12292
  23.7 10.7 %copy-start.3 = (s32[1024,1]{0,1:T(1,128)S(1)}, s32[1024,1]{0,1:T(1,128)}, u32[]{:S(2)}) copy-start(s32[1024,1]{0,1:T(1,128)} %param.9) | copy-start | bytes 12292
  27.6 88.8 %all-to-all-start.1 = ((bf16[1024,8,128]{0,2,1:T(8,128)(2,1)}), bf16[1024,8,128]{0,2,1:T(8,128)(2,1)}, u32[]{:S(2)}, u32[]{:S(2)}) async-start(bf16[1024,8,128]{0,2,1:T(8,128)(2,1)} %bitcast.35), calls=%async_computation.1 | async-start | bytes 4194304 | tf_op jit(solution)/shard_map/all_to_all | solution.py:71
  73.8 4.9 %copy-start.1 = (s32[512]{0:T(512)S(1)}, s32[512]{0:T(512)}, u32[]{:S(2)}) copy-start(s32[512]{0:T(512)} %param.10) | copy-start | bytes 6148
  188.1 7.0 %copy-start.4 = (bf16[4,128]{1,0:T(4,128)(2,1)S(1)}, bf16[4,128]{1,0:T(4,128)(2,1)}, u32[]{:S(2)}) copy-start(bf16[4,128]{1,0:T(4,128)(2,1)} %param.15) | copy-start | bytes 3076
  188.1 79.3 %all-to-all-start.2 = ((bf16[16,1024,128]{2,1,0:T(8,128)(2,1)}), bf16[16,1024,128]{2,1,0:T(8,128)(2,1)}, u32[]{:S(2)}, u32[]{:S(2)}) async-start(bf16[16,1024,128]{2,1,0:T(8,128)(2,1)} %broadcast_select_fusion), calls=%async_computation.2 | async-start | bytes 8388608 | tf_op jit(solution)/shard_map/all_to_all | solution.py:80
  195.0 110.6 %reduce-scatter.2.cloned.1.call-start = ((), (), s32[]{:S(2)}) async-start(), calls=%async_computation.4 | async-start | bytes 2359296 | tf_op jit(solution)/shard_map/reduce_scatter | solution.py:89
Sparse Core Ops, SparseCore 0:
  272.6 32.9 reduce-scatter.1
where the time goes:
time: 326 us; the launch traced here: 323 us
  blocking collectives  116 us (36%)
  local copies, waits for them, and re-layouts  103 us (32%)
  matrix products  33.8 us (10%)
  waiting for transfers between devices  22 us (7%)
  other arithmetic  20.2 us (6%)
  between operations  14.2 us (4%)
  starting transfers between devices  13.8 us (4%)
    all_gather x1, blocking collectives, shards(): all_queries = lax.all_gather(queries, 'wide', axis=0, tiled=True)  72.3 us
    gather x1, local copies, waits for them, and re-layouts, shards(): jnp.take(padded, source, axis=0).reshape(wide_count, per_owner, piece)  57.4 us
    all_gather x1, blocking collectives, shards(): block_ids = lax.all_gather(cluster_ids[:, 0], 'narrow', axis=0, tiled=True)  32.9 us
    scatter x1, local copies, waits for them, and re-layouts, shards(): source = jnp.full((slot_capacity,), block_rows, jnp.int32).at[flat_slot]....  30.5 us
    reduce_scatter x1, waiting for transfers between devices, shards(): lax.psum_scatter(lax.dot_general(all_queries, owned_items, (((1,), (1,)),...  21.9 us
    all_to_all x1, blocking collectives, shards(): lax.all_to_all(slot_counts.astype(jnp.bfloat16), 'wide', split_axis=0, co...  10.8 us
    dot_general x1, matrix products, shards(): raw = jnp.dot(second, w_third, preferred_element_type=jnp.float32)  9.81 us
    select_n x1, other arithmetic, shards(): jnp.take(padded, source, axis=0).reshape(wide_count, per_owner, piece)  7.63 us
  transfers between devices with their start and end apart: 3, of which 1 were waited for; matrix products, arithmetic and copies ran while one was open for 15% of the time, Pallas kernels for 0%

commit v1 on v0

v1 whole, which is shorter than its diff:
```python
import functools
import math

import jax
import jax.numpy as jnp
from jax import lax
from jax.experimental import pallas as pl
from jax.experimental.pallas import tpu as pltpu
from jax.sharding import PartitionSpec as P

MESH = pl.DeviceIdType.MESH
CL_DEV = 32
MOST = 32
WIDE = 16
NARROW = 8
ROWS = 1024
PIECE = 128
SLOTS = 512
CHUNKS = 4
CHUNK = ROWS // CHUNKS
BLOCKS = NARROW * CHUNK // 128
CAP = 208
TAIL = CAP - 128
SELF = 2
NT = (((1,), (1,)), ((), ()))
F32 = jnp.float32
BF16 = jnp.bfloat16


def silu(v):
    half = 0.5 * v
    return half + half * jnp.tanh(half)


def loop(low, high, body):
    def step(i, carry):
        body(i)
        return carry

    lax.fori_loop(low, high, step, 0)


def peer_step(i):
    return i + (i + 13) // 15


def iota(shape, dim):
    return lax.broadcasted_iota(jnp.int32, shape, dim)


def exchange(
    feats_hbm, w1_hbm, w2_hbm, w3_hbm, gain_ref, ids_ref, slots_ref, query_ref,
    arrived_ref, tags_ref, best_ref,
    feats, w1, w2, w3, emb, land, rhs, stage, tag_out, ids_all, owner_of, levels, ranks, dest, dest_carry, spill,
    q_wide, q_mine, q_all, perm, ends, table, table_in, final, final_in,
    load_sem, ids_s, ids_r, qw_s, qw_r, qn_s, qn_r, emb_s, emb_r, data_s, data_r, tag_s, tag_r,
    table_s, table_r, final_s, final_r, own_sem,
):
    w = lax.axis_index("wide")
    n = lax.axis_index("narrow")

    def wide_peer(k):
        down = (2 + k) % 4
        across = (2 + k + k // 4) % 4
        return ((w // 4 + down) % 4) * 4 + (w % 4 + across) % 4

    def narrow_peer(d):
        return (n + d) % NARROW

    def remote(src, dst, send, recv, device):
        return pltpu.make_async_remote_copy(
            src_ref=src, dst_ref=dst, send_sem=send, recv_sem=recv, device_id=device, device_id_type=MESH
        )

    def ids_copy(d):
        return remote(ids_ref, ids_all.at[n], ids_s.at[d], ids_r.at[d], (w, narrow_peer(d)))

    def q_wide_copy(k):
        return remote(query_ref, q_wide.at[w], qw_s.at[k], qw_r.at[k], (wide_peer(k), n))

    def q_narrow_copy(d):
        return remote(q_mine, q_all.at[n], qn_s.at[d], qn_r.at[d], (w, narrow_peer(d)))

    def rows_of(c):
        return pl.ds(pl.multiple_of(c * CHUNK, CHUNK), CHUNK)

    def emb_copy(c, d):
        to = narrow_peer(d)
        return remote(
            emb.at[to, rows_of(c)], land.at[n, rows_of(c)], emb_s.at[c, d], emb_r.at[c, d], (w, to)
        )

    def slab_rows(c):
        return pl.ds(pl.multiple_of(c * CAP, 16), CAP)

    def data_copy(c, k):
        return remote(
            stage.at[c, k], arrived_ref.at[w, slab_rows(c)], data_s.at[c, k], data_r.at[c, k], (wide_peer(k), n)
        )

    def tag_copy(k):
        return remote(tag_out.at[k], tags_ref.at[w], tag_s.at[k], tag_r.at[k], (wide_peer(k), n))

    def table_copy(d):
        to = narrow_peer(d)
        return remote(table.at[to], table_in.at[n], table_s.at[d], table_r.at[d], (w, to))

    def final_copy(k):
        to = wide_peer(k)
        return remote(final.at[to], final_in.at[w], final_s.at[k], final_r.at[k], (to, n))

    def own_data(c):
        return pltpu.make_async_copy(stage.at[c, SELF], arrived_ref.at[w, slab_rows(c)], own_sem.at[c])

    def own_tag():
        return pltpu.make_async_copy(tag_out.at[SELF], tags_ref.at[w], own_sem.at[CHUNKS])

    loads = [
        pltpu.make_async_copy(src, dst, load_sem.at[i])
        for i, (src, dst) in enumerate(((feats_hbm, feats), (w1_hbm, w1), (w2_hbm, w2), (w3_hbm, w3)))
    ]
    for load in loads:
        load.start()

    barrier = pltpu.get_barrier_semaphore()

    def greet_wide(i):
        pl.semaphore_signal(barrier, inc=1, device_id=(wide_peer(peer_step(i)), n), device_id_type=MESH)

    def greet_narrow(d):
        pl.semaphore_signal(barrier, inc=1, device_id=(w, narrow_peer(d)), device_id_type=MESH)

    loop(1, NARROW, greet_narrow)
    loop(0, WIDE - 1, greet_wide)

    slot_level = iota((SLOTS, SLOTS), 0)
    cluster_level = iota((SLOTS, SLOTS), 1).astype(F32)
    holder = jnp.sum(jnp.where(slots_ref[...] == slot_level, cluster_level, 0.0), axis=1, keepdims=True)
    owner_of[...] = jnp.broadcast_to(holder, (SLOTS, 128)).astype(jnp.int32)
    place = (iota((SLOTS, 128), 0) % CL_DEV * MOST).astype(F32)
    levels[...] = place
    ranks[...] = jnp.zeros_like(ranks)
    dest_carry[...] = jnp.zeros_like(dest_carry)
    ids_all[n] = ids_ref[...]
    q_wide[w] = query_ref[...]

    pl.semaphore_wait(barrier, NARROW - 1 + WIDE - 1)
    loop(1, NARROW, lambda d: ids_copy(d).start())
    loop(0, WIDE - 1, lambda i: q_wide_copy(peer_step(i)).start())
    for load in loads:
        load.wait()

    def tower(c):
        x = feats[rows_of(c), :]
        first = silu(jnp.dot(x, w1[...], preferred_element_type=F32)).astype(BF16)
        second = silu(jnp.dot(first, w2[...], preferred_element_type=F32)).astype(BF16)
        raw = jnp.dot(second, w3[...], preferred_element_type=F32)
        scale = lax.rsqrt(jnp.mean(raw * raw, axis=1, keepdims=True) + 1e-06)
        embedding = (raw * scale * gain_ref[...]).astype(BF16)
        for j in range(NARROW):
            emb[j, rows_of(c), :] = embedding[:, j * PIECE : (j + 1) * PIECE]
        land[n, rows_of(c), :] = emb[n, rows_of(c), :]
        loop(1, NARROW, lambda d: emb_copy(c, d).start())

    def place_rows():
        loop(1, NARROW, lambda d: ids_copy(d).wait_recv())
        upto = iota((128, 256), 0) <= iota((128, 256), 1)
        sums = upto.astype(F32).astype(BF16)

        def source(m):
            for k in range(8):
                c = k * 128 // CHUNK
                q = m * (CHUNK // 128) + k % (CHUNK // 128)
                row = ids_all[m, k : k + 1, :]
                named = owner_of[...] == row
                onehot = jnp.where(named, 1.0, 0.0)
                counts = jnp.dot(onehot.astype(BF16), sums, preferred_element_type=F32)
                where = jnp.where(named, counts[:, :128] + levels[...], 0.0)
                ranks[c, pl.ds(q, 1), :] = jnp.sum(where, axis=0, keepdims=True)
                levels[...] += counts[:, 128:]
                owned = jnp.sum(onehot.reshape(WIDE, CL_DEV, 128), axis=1)
                ordered = jnp.dot(owned.astype(BF16), sums, preferred_element_type=F32)
                dest[c, q] = jnp.where(owned > 0.0, ordered[:, :128] + dest_carry[c] - 1.0, -1.0)
                dest_carry[c] += ordered[:, 128:]

        loop(0, NARROW, source)
        most = jnp.max(dest_carry[...].reshape(CHUNKS * WIDE, 128), axis=0, keepdims=True)
        spill[...] = jnp.broadcast_to(jnp.where(most > float(CAP), 1.0, 0.0), spill.shape)

        loop(0, WIDE - 1, lambda i: q_wide_copy(peer_step(i)).wait_recv())
        at = iota((4 * WIDE, 8 * WIDE), 0)
        pick = iota((4 * WIDE, 8 * WIDE), 1) == at // 4 * 8 + at % 4
        spread = q_wide[...].reshape(8 * WIDE, PIECE).astype(BF16)
        q_mine[...] = jnp.dot(pick.astype(F32).astype(BF16), spread, preferred_element_type=F32).astype(BF16)
        q_all[n] = q_mine[...]
        loop(1, NARROW, lambda d: q_narrow_copy(d).start())

    def pack(c):
        loop(1, NARROW, lambda d: emb_copy(c, d).wait_recv())
        turned = jnp.transpose(ranks[c])
        left = iota((128, 128), 1) < 64
        for q in range(BLOCKS):
            m, part = q // (CHUNK // 128), q % (CHUNK // 128)
            start = pl.multiple_of(c * CHUNK + part * 128, 128)
            rhs[q * 128 : (q + 1) * 128, 0:128] = land[m, pl.ds(start, 128), :]
            column = jnp.broadcast_to(turned[:, q : q + 1], (128, 128))
            high = jnp.floor(column * (1.0 / 32.0)) * 32.0
            rhs[q * 128 : (q + 1) * 128, 128:256] = jnp.where(left, high, column - high).astype(BF16)

        spot = iota((CAP, 128), 0).astype(F32)
        eye = iota((128, 128), 0) == iota((128, 128), 1)
        eye_tail = iota((TAIL, 128), 0) == iota((TAIL, 128), 1)
        last_lane = iota((1, 128), 1) == 127

        def to_owner(k):
            to = wide_peer(k)
            parts = []
            for q in range(BLOCKS):
                row = dest[c, q, pl.ds(to, 1), :]
                parts.append(jnp.where(spot == row, 1.0, 0.0).astype(BF16))
            onehot = jnp.concatenate(parts, axis=1)
            packed = jnp.dot(onehot, rhs[...], preferred_element_type=F32)
            stage[c, k] = packed[:, :128].astype(BF16)
            tag = packed[:, 128:]
            tag = tag + pltpu.roll(tag, 64, 1)
            upper = jnp.sum(jnp.where(eye, tag[:128], 0.0), axis=0, keepdims=True)
            lower = jnp.sum(jnp.where(eye_tail, tag[128:], 0.0), axis=0, keepdims=True)
            tag_out[k, pl.ds(2 * c, 1), :] = upper
            tag_out[k, pl.ds(2 * c + 1, 1), :] = lower + jnp.where(last_lane, spill[0:1, :], 0.0)

            @pl.when(k != SELF)
            def _():
                data_copy(c, k).start()

                @pl.when(c == CHUNKS - 1)
                def _():
                    tag_copy(k).start()

            @pl.when(k == SELF)
            def _():
                own_data(c).start()

                @pl.when(c == CHUNKS - 1)
                def _():
                    own_tag().start()

        loop(0, WIDE, to_owner)

    def turn(t):
        @pl.when(t < CHUNKS)
        def _():
            tower(t)

        @pl.when(t == 0)
        def _():
            place_rows()

        @pl.when(t >= 1)
        def _():
            pack(t - 1)

    loop(0, CHUNKS + 1, turn)

    loop(1, NARROW, lambda d: q_narrow_copy(d).wait_recv())
    score = jnp.zeros((4 * WIDE, ROWS), F32)
    for j in range(NARROW):
        score += lax.dot_general(q_all[j], emb[j], NT, preferred_element_type=F32)
    ids_f = ids_ref[...].astype(F32)
    id_row = jnp.concatenate([ids_f[k : k + 1, :] for k in range(8)], axis=1)
    key_row = id_row * float(ROWS) + iota((1, ROWS), 1).astype(F32)
    eye = iota((128, 128), 0) == iota((128, 128), 1)
    order = iota((128, ROWS), 1).astype(F32)
    for k in range(8):
        key = jnp.sum(jnp.where(eye, key_row[:, k * 128 : (k + 1) * 128], 0.0), axis=1, keepdims=True)
        position = jnp.sum(jnp.where(key_row < key, 1.0, 0.0), axis=1, keepdims=True)
        perm[k * 128 : (k + 1) * 128, :] = jnp.where(order == position, 1.0, 0.0).astype(BF16)
    high = score.astype(BF16)
    low = (score - high.astype(F32)).astype(BF16)
    id_high = jnp.floor(id_row * (1.0 / 32.0)) * 32.0
    line = iota((16, ROWS), 0)
    extra = jnp.where(line == 0, id_high, jnp.where(line == 1, id_row - id_high, 0.0)).astype(BF16)
    arranged = jnp.dot(jnp.concatenate([high, low, extra], axis=0), perm[...], preferred_element_type=F32)
    top = arranged[0:64] + arranged[64:128]
    seg = jnp.broadcast_to(arranged[128:129] + arranged[129:130], (8, ROWS))
    lane = iota((8, ROWS), 1)
    for step in (1, 2, 4, 8, 16):
        same = (pltpu.roll(seg, step, 1) == seg) & (lane >= step)
        gate = jnp.where(same, 0.0, -jnp.inf)[0:1]
        top = jnp.maximum(top, pltpu.roll(top, step, 1) + gate)
    closing = (pltpu.roll(seg, ROWS - 1, 1) != seg) | (lane == ROWS - 1)
    end_id = jnp.where(closing, seg, -1.0)[0:1]
    for k in range(ROWS // 128):
        match = owner_of[...].astype(F32) == end_id[:, k * 128 : (k + 1) * 128]
        ends[:, k * 128 : (k + 1) * 128] = jnp.where(match, 1.0, 0.0).astype(BF16)
    high = top.astype(BF16)
    low = (top - high.astype(F32)).astype(BF16)
    ones = jnp.ones((16, ROWS), BF16)
    found = lax.dot_general(jnp.concatenate([high, low, ones], axis=0), ends[...], NT, preferred_element_type=F32)
    by_slot = jnp.where(found[128:129] > 0.0, found[0:64] + found[64:128], -jnp.inf)
    for j in range(NARROW):
        table[j] = by_slot[8 * j : 8 * j + 8]
    table_in[n] = table[n]
    loop(1, NARROW, lambda d: table_copy(d).start())
    loop(1, NARROW, lambda d: table_copy(d).wait_recv())
    merged = jnp.max(table_in[...], axis=0)
    for o in range(WIDE):
        group = merged[:, o // 4 * 128 : o // 4 * 128 + 128]
        final[o] = pltpu.roll(group, (128 - 32 * (o % 4)) % 128, 1) if o % 4 else group
    final_in[w] = final[w]
    loop(0, WIDE - 1, lambda i: final_copy(peer_step(i)).start())
    loop(0, WIDE - 1, lambda i: final_copy(peer_step(i)).wait_recv())
    best_ref[...] = jnp.max(final_in[...], axis=0)

    def settle_wide(i):
        k = peer_step(i)
        q_wide_copy(k).wait_send()
        final_copy(k).wait_send()
        tag_copy(k).wait()

    def settle_narrow(d):
        ids_copy(d).wait_send()
        q_narrow_copy(d).wait_send()
        table_copy(d).wait_send()

    loop(0, WIDE - 1, settle_wide)
    loop(1, NARROW, settle_narrow)

    def settle_chunk(c):
        loop(1, NARROW, lambda d: emb_copy(c, d).wait_send())
        loop(0, WIDE - 1, lambda i: data_copy(c, peer_step(i)).wait())
        own_data(c).wait()

    loop(0, CHUNKS, settle_chunk)
    own_tag().wait()


def run_exchange(features, w_first, w_second, w_third, gain, ids, slots, queries):
    vmem = pl.BlockSpec(memory_space=pltpu.VMEM)
    anywhere = pl.BlockSpec(memory_space=pl.ANY)
    dma = pltpu.SemaphoreType.DMA
    return pl.pallas_call(
        exchange,
        out_shape=(
            jax.ShapeDtypeStruct((WIDE, CHUNKS * CAP, PIECE), BF16),
            jax.ShapeDtypeStruct((WIDE, 8, 128), F32),
            jax.ShapeDtypeStruct((8, 128), F32),
        ),
        in_specs=[anywhere] * 4 + [vmem] * 4,
        out_specs=(anywhere, anywhere, vmem),
        scratch_shapes=[
            pltpu.VMEM((ROWS, 1024), BF16),
            pltpu.VMEM((1024, 1024), BF16),
            pltpu.VMEM((1024, 1024), BF16),
            pltpu.VMEM((1024, 1024), BF16),
            pltpu.VMEM((NARROW, ROWS, PIECE), BF16),
            pltpu.VMEM((NARROW, ROWS, PIECE), BF16),
            pltpu.VMEM((NARROW * CHUNK, 256), BF16),
            pltpu.VMEM((CHUNKS, WIDE, CAP, PIECE), BF16),
            pltpu.VMEM((WIDE, 8, 128), F32),
            pltpu.VMEM((NARROW, 8, 128), jnp.int32),
            pltpu.VMEM((SLOTS, 128), jnp.int32),
            pltpu.VMEM((SLOTS, 128), F32),
            pltpu.VMEM((CHUNKS, 128, 128), F32),
            pltpu.VMEM((CHUNKS, BLOCKS, WIDE, 128), F32),
            pltpu.VMEM((CHUNKS, WIDE, 128), F32),
            pltpu.VMEM((8, 128), F32),
            pltpu.VMEM((WIDE, 8, PIECE), F32),
            pltpu.VMEM((4 * WIDE, PIECE), BF16),
            pltpu.VMEM((NARROW, 4 * WIDE, PIECE), BF16),
            pltpu.VMEM((ROWS, ROWS), BF16),
            pltpu.VMEM((SLOTS, ROWS), BF16),
            pltpu.VMEM((NARROW, 8, SLOTS), F32),
            pltpu.VMEM((NARROW, 8, SLOTS), F32),
            pltpu.VMEM((WIDE, 8, 128), F32),
            pltpu.VMEM((WIDE, 8, 128), F32),
            dma((4,)),
            dma((NARROW,)), dma((NARROW,)),
            dma((WIDE,)), dma((WIDE,)),
            dma((NARROW,)), dma((NARROW,)),
            dma((CHUNKS, NARROW)), dma((CHUNKS, NARROW)),
            dma((CHUNKS, WIDE)), dma((CHUNKS, WIDE)),
            dma((WIDE,)), dma((WIDE,)),
            dma((NARROW,)), dma((NARROW,)),
            dma((WIDE,)), dma((WIDE,)),
            dma((CHUNKS + 1,)),
        ],
        compiler_params=pltpu.CompilerParams(
            collective_id=0, has_side_effects=True, vmem_limit_bytes=56 * 2**20
        ),
        name="exchange",
    )(features, w_first, w_second, w_third, gain, ids, slots, queries)


def unpack(arrived_ref, tags_ref, slab_ref):
    spot = iota((CL_DEV * MOST, 1), 0).astype(F32) + 1.0
    total = jnp.zeros((CL_DEV * MOST, PIECE), F32)
    for c in range(CHUNKS):
        row = jnp.concatenate([tags_ref[0, 2 * c : 2 * c + 1, :], tags_ref[0, 2 * c + 1 : 2 * c + 2, :TAIL]], axis=1)
        onehot = jnp.where(spot == row, 1.0, 0.0).astype(BF16)
        total += jnp.dot(onehot, arrived_ref[0, c * CAP : (c + 1) * CAP, :], preferred_element_type=F32)
    slab_ref[0] = total.astype(BF16)


def run_unpack(arrived, tags):
    return pl.pallas_call(
        unpack,
        grid=(WIDE,),
        out_shape=jax.ShapeDtypeStruct((WIDE, CL_DEV * MOST, PIECE), BF16),
        in_specs=[
            pl.BlockSpec((1, CHUNKS * CAP, PIECE), lambda b: (b, 0, 0)),
            pl.BlockSpec((1, 8, 128), lambda b: (b, 0, 0)),
        ],
        out_specs=pl.BlockSpec((1, CL_DEV * MOST, PIECE), lambda b: (b, 0, 0)),
        compiler_params=pltpu.CompilerParams(vmem_limit_bytes=32 * 2**20),
        name="unpack",
    )(arrived, tags)


def slot_table(id_list, cluster_slots, total):
    levels = jnp.arange(total, dtype=jnp.int32)
    onehot = (id_list[:, None] == levels[None, :]).astype(jnp.bfloat16)
    high_part = (cluster_slots // 64).astype(jnp.bfloat16)
    low_part = (cluster_slots % 64).astype(jnp.bfloat16)
    slot_value = 64.0 * jnp.dot(onehot, high_part, preferred_element_type=jnp.float32) + jnp.dot(
        onehot, low_part, preferred_element_type=jnp.float32
    )
    return (onehot, slot_value.astype(jnp.int32))


def cluster_ranks(onehot):
    count, total = onehot.shape
    block = math.gcd(count, 256)
    number = count // block
    stacked = onehot.reshape(number, block, total)
    inner = jnp.arange(block, dtype=jnp.int32)
    lower = (inner[:, None] >= inner[None, :]).astype(jnp.bfloat16)
    inside = jnp.einsum("rs,bsc->brc", lower, stacked, preferred_element_type=jnp.float32)
    block_sums = inside[:, -1, :]
    outer = jnp.arange(number, dtype=jnp.int32)
    before = (outer[:, None] > outer[None, :]).astype(jnp.float32)
    earlier = jnp.dot(
        before, block_sums, precision=lax.Precision.HIGHEST, preferred_element_type=jnp.float32
    )
    position = jnp.sum(stacked * (inside - 1.0 + earlier[:, None, :]), axis=2)
    return (position.reshape(count).astype(jnp.int32), jnp.sum(block_sums, axis=0))


def padded_slab(features, cluster_ids, cluster_slots, w_first, w_second, w_third, emb_gain):
    first = jax.nn.silu(jnp.dot(features, w_first, preferred_element_type=F32)).astype(BF16)
    second = jax.nn.silu(jnp.dot(first, w_second, preferred_element_type=F32)).astype(BF16)
    raw = jnp.dot(second, w_third, preferred_element_type=F32)
    scale = lax.rsqrt(jnp.mean(raw * raw, axis=1, keepdims=True) + 1e-06)
    embedding = (raw * scale * emb_gain).astype(BF16)
    block_ids = lax.all_gather(cluster_ids[:, 0], "narrow", axis=0, tiled=True)
    block_rows = block_ids.shape[0]
    onehot, slot_of = slot_table(block_ids, cluster_slots, SLOTS)
    positions, _ = cluster_ranks(onehot)
    flat_slot = slot_of * MOST + positions
    sliced = lax.all_to_all(embedding, "narrow", split_axis=1, concat_axis=0, tiled=True)
    source = (
        jnp.full((SLOTS * MOST,), block_rows, jnp.int32)
        .at[flat_slot]
        .set(jnp.arange(block_rows, dtype=jnp.int32))
    )
    padded = jnp.concatenate([sliced, jnp.zeros((1, PIECE), BF16)], axis=0)
    outgoing = jnp.take(padded, source, axis=0).reshape(WIDE, CL_DEV * MOST, PIECE)
    return lax.all_to_all(outgoing, "wide", split_axis=0, concat_axis=0, tiled=True)


def shards(features, cluster_ids, cluster_slots, w_first, w_second, w_third, emb_gain, queries):
    ids = cluster_ids.reshape(8, 128)
    query = jnp.pad(queries.astype(F32), ((0, 4), (0, 0)))
    arrived, tags, best = run_exchange(
        features, w_first, w_second, w_third, emb_gain.reshape(1, 1024), ids, cluster_slots.reshape(1, SLOTS), query
    )
    fits = jnp.max(tags[:, 7, 127]) == 0.0
    slab = lax.cond(
        fits,
        lambda: run_unpack(arrived, tags),
        lambda: padded_slab(features, cluster_ids, cluster_slots, w_first, w_second, w_third, emb_gain),
    )
    return (best[:, :CL_DEV], slab.reshape(WIDE, CL_DEV, MOST, PIECE))


def solution(mesh):
    placed = (
        P(("wide", "narrow"), None),
        P(("wide", "narrow"), None),
        P(),
        P(),
        P(),
        P(),
        P(),
        P("wide", "narrow"),
    )
    return jax.shard_map(
        shards,
        mesh=mesh,
        in_specs=placed,
        out_specs=(P("narrow", "wide"), P(None, "wide", None, "narrow")),
        check_vma=False,
    )
```

time: 326 us -> 103 us (0.32)
  blocking collectives: 116 us -> 0 us
  local copies, waits for them, and re-layouts: 103 us -> 5.74 us
  Pallas kernels: 0 us -> 93.5 us
  matrix products: 33.8 us -> 0 us
  waiting for transfers between devices: 22 us -> 0 us
  other arithmetic: 20.2 us -> 1.96 us
  starting transfers between devices: 13.8 us -> 0 us
  between operations: 14.2 us -> 1.34 us
    all_gather x2 -> x0, blocking collectives: 105 us -> none  [the longest x1 72.3 us: shards(): all_queries = lax.all_gather(queries, 'wide', axis=0, tiled=True)]
    pallas_call x0 -> x2, Pallas kernels: none -> 93.5 us  [the longest x1 78 us: run_exchange(): pl.pallas_call(exchange, out_shape=(jax.ShapeDtypeStruct((WIDE, CHUNKS *...]
    gather x1 -> x0, local copies, waits for them, and re-layouts: 57.4 us -> none  [shards(): jnp.take(padded, source, axis=0).reshape(wide_count, per_owner, piece)]
    dot_general x7 -> x0, matrix products: 33.8 us -> none  [the longest x1 9.81 us: shards(): raw = jnp.dot(second, w_third, preferred_element_type=jnp.float32)]
    scatter x1 -> x0, local copies, waits for them, and re-layouts: 30.5 us -> none  [shards(): source = jnp.full((slot_capacity,), block_rows, jnp.int32).at[flat_slot]....]
    reduce_scatter x1 -> x0, waiting for transfers between devices: 21.9 us -> none  [shards(): lax.psum_scatter(lax.dot_general(all_queries, owned_items, (((1,), (1,)),...]
    all_to_all x2 -> x0, starting transfers between devices: 13.7 us -> none  [the longest x1 6.93 us: shards(): lax.all_to_all(outgoing, 'wide', split_axis=0, concat_axis=0, tiled=True)]
    all_to_all x1 -> x0, blocking collectives: 10.8 us -> none  [shards(): lax.all_to_all(slot_counts.astype(jnp.bfloat16), 'wide', split_axis=0, co...]
  transfers between devices with their start and end apart: 3 -> 0, of which waited for: 1 -> 0; matrix products, arithmetic and copies ran while one was open for 15% -> 0% of each run, Pallas kernels for 0% -> 0%
where the time goes in v1:
time: 103 us
  Pallas kernels  93.5 us (91%)
  local copies, waits for them, and re-layouts  5.74 us (6%)
  other arithmetic  1.96 us (2%)
  between operations  1.34 us (1%)
    pallas_call x1, Pallas kernels, run_exchange(): pl.pallas_call(exchange, out_shape=(jax.ShapeDtypeStruct((WIDE, CHUNKS *...  78 us
    pallas_call x1, Pallas kernels, run_unpack(): pl.pallas_call(unpack, grid=(WIDE,), out_shape=jax.ShapeDtypeStruct((WIDE...  15.5 us
    unnamed x12, local copies, waits for them, and re-layouts  5.74 us

profile of v1, /device:TPU:1, one launch (start us, length us, event | category | flops | bytes accessed | tf_op | source)
XLA Modules:
  0.0 102.7 jit_solution(17269491553113467314)
XLA Ops:
  0.6 1.3 %pad_convert_fusion.query_ref = f32[8,128]{1,0:T(8,128)} fusion(bf16[4,128]{1,0:T(4,128)(2,1)} %param.17), kind=kLoop, calls=%fused_computation.46 | loop fusion | flops 1024 | bytes 5120 | tf_op jit(solution)/shard_map/jit(_pad)/pad | solution.py:472
  1.9 0.0 copy-start
  1.9 0.0 copy-start.1
  1.9 0.0 copy-start.2
  1.9 0.0 copy-start.3
  1.9 78.0 %exchange.1 = (bf16[16,832,128]{2,1,0:T(8,128)(2,1)}, f32[16,8,128]{2,1,0:T(8,128)S(1)}, f32[8,128]{1,0:T(8,128)}) custom-call(bf16[1024,1024]{1,0:T(8,128)(2,1)} %feats_hbm.1, bf16[1024,1024]{1,0:T(8,128)(2,1)} %w1_hbm.1, bf16[1024,1024]{1,0:T(8,128)(2,1)} %w2_hbm.1, bf16[1024,1024]{1,0:T(8,128)(2,1)} %w3_hbm.1, f32[1,1024]{1,0:T(1,128)} %bitcast.42, ...), custom_call_target="tpu_custom_call" | custom-call | tf_op jit(solution)/shard_map/exchange/pallas_call | solution.py:341
  79.9 0.7 slice_reduce_fusion
  81.3 0.0 copy-done
  81.3 0.0 copy-done.1
  81.3 0.0 copy-done.2
  81.3 0.0 copy-done.3
  81.3 0.0 copy-start.4
  81.3 15.7 %conditional.1 = (bf16[16,32,32,128]{3,2,1,0:T(8,128)(2,1)}) conditional(s32[]{:T(128)} %convert_element_type.39, (s32[1024,1]{0,1:T(1,128)S(1)}, s32[512]{0:T(512)S(1)}, bf16[1024,1024]{1,0:T(8,128)(2,1)S(1)}, bf16[1024,1024]{1,0:T(8,128)(2,1)}, bf16[1024,1024]{1,0:T(8,128)(2,1)}, /*index=5*/bf16[1024,1024]{1,0:T(8,128)(2,1)}, ...), branch_computations={%region_1.5_spmd, %region_5.6_spmd} | conditional | flops 8673079296 | bytes 102107448 | solution.py:477
  81.6 15.5 %unpack.1 = bf16[16,1024,128]{2,1,0:T(8,128)(2,1)} custom-call(bf16[16,832,128]{2,1,0:T(8,128)(2,1)} %get-tuple-element.29.arrived_ref, f32[16,8,128]{2,1,0:T(8,128)S(1)} %get-tuple-element.30.tags_ref), custom_call_target="tpu_custom_call" | custom-call | tf_op jit(solution)/shard_map/cond/branch_1_fun/unpack/pallas_call | solution.py:405
  97.0 0.0 copy-done.4
  97.0 0.6 copy.21
  97.6 5.1 %copy.22 = bf16[16,32,32,128]{3,2,1,0:T(8,128)(2,1)} copy(bf16[16,32,32,128]{3,2,1,0:T(8,128)(2,1)} %get-tuple-element.47) | data formatting | bytes 8388608
Async XLA Ops:
  1.9 79.4 %copy-start = (bf16[1024,1024]{1,0:T(8,128)(2,1)S(1)}, bf16[1024,1024]{1,0:T(8,128)(2,1)}, u32[]{:S(2)}) copy-start(bf16[1024,1024]{1,0:T(8,128)(2,1)} %feats_hbm.1) | copy-start | bytes 6291460
  1.9 79.4 %copy-start.1 = (f32[1024]{0:T(1024)S(1)}, f32[1024]{0:T(1024)}, u32[]{:S(2)}) copy-start(f32[1024]{0:T(1024)} %param.16) | copy-start | bytes 12292
  1.9 79.4 %copy-start.2 = (s32[1024,1]{0,1:T(1,128)S(1)}, s32[1024,1]{0,1:T(1,128)}, u32[]{:S(2)}) copy-start(s32[1024,1]{0,1:T(1,128)} %param.11) | copy-start | bytes 12292
  1.9 79.4 %copy-start.3 = (s32[512]{0:T(512)S(1)}, s32[512]{0:T(512)}, u32[]{:S(2)}) copy-start(s32[512]{0:T(512)} %param.12) | copy-start | bytes 6148
  81.3 15.7 %copy-start.4 = (f32[8,128]{1,0:T(8,128)S(1)}, f32[8,128]{1,0:T(8,128)}, u32[]{:S(2)}) copy-start(f32[8,128]{1,0:T(8,128)} %get-tuple-element.36) | copy-start | bytes 12292

commit v2 on v1

v2 whole, which is shorter than its diff:
```python
import functools
import math

import jax
import jax.numpy as jnp
from jax import lax
from jax.experimental import pallas as pl
from jax.experimental.pallas import tpu as pltpu
from jax.sharding import PartitionSpec as P

MESH = pl.DeviceIdType.MESH
CL_DEV = 32
MOST = 32
WIDE = 16
NARROW = 8
ROWS = 1024
PIECE = 128
SLOTS = 512
SIZES = (256, 256, 256, 256)
CAPS = (176, 176, 176, 176, 48)
CHUNKS = len(SIZES)
GROUPS = CHUNKS + 1
STARTS = tuple(sum(SIZES[:c]) for c in range(CHUNKS))
OFFSETS = tuple(sum(CAPS[:g]) for g in range(GROUPS))
TOTAL = sum(CAPS)
BLOCKS = NARROW * ROWS // 128
SELF = 2
BATCH = 4
NT = (((1,), (1,)), ((), ()))
F32 = jnp.float32
BF16 = jnp.bfloat16


def silu(v):
    half = 0.5 * v
    return half + half * jnp.tanh(half)


def loop(low, high, body):
    def step(i, carry):
        body(i)
        return carry

    lax.fori_loop(low, high, step, 0)


def peer_step(i):
    return i + (i + 13) // 15


def iota(shape, dim):
    return lax.broadcasted_iota(jnp.int32, shape, dim)


def exchange(
    feats_hbm, w1_hbm, w2_hbm, w3_hbm, gain_ref, ids_ref, slots_ref, query_ref,
    arrived_ref, tags_ref, best_ref,
    feats, w1, w2, w3, emb, rhs, stage, tag_out, ids_all, owner_of, levels, ranks, dest, dest_over, dest_carry, spill, over_sum,
    q_wide, q_mine, q_all, perm, ends, table, table_in, final, final_in,
    load_sem, ids_s, ids_r, qw_s, qw_r, qn_s, qn_r, emb_s, emb_r, data_s, data_r, tag_s, tag_r,
    table_s, table_r, final_s, final_r, own_sem, own_tag_sem,
):
    w = lax.axis_index("wide")
    n = lax.axis_index("narrow")

    def wide_peer(k):
        down = (2 + k) % 4
        across = (2 + k + k // 4) % 4
        return ((w // 4 + down) % 4) * 4 + (w % 4 + across) % 4

    def narrow_peer(d):
        return (n + d) % NARROW

    def remote(src, dst, send, recv, device):
        return pltpu.make_async_remote_copy(
            src_ref=src, dst_ref=dst, send_sem=send, recv_sem=recv, device_id=device, device_id_type=MESH
        )

    def ids_copy(d):
        return remote(ids_ref, ids_all.at[n], ids_s.at[d], ids_r.at[d], (w, narrow_peer(d)))

    def q_wide_copy(k):
        return remote(query_ref, q_wide.at[w], qw_s.at[k], qw_r.at[k], (wide_peer(k), n))

    def q_narrow_copy(d):
        return remote(q_mine, q_all.at[n], qn_s.at[d], qn_r.at[d], (w, narrow_peer(d)))

    def rows_of(c):
        return pl.ds(STARTS[c], SIZES[c])

    def landing(c, m):
        start = NARROW * STARTS[c] + m * SIZES[c]
        return rhs.at[pl.ds(pl.multiple_of(start, 128), SIZES[c]), pl.ds(0, 128)]

    def emb_copy(c, d):
        to = narrow_peer(d)
        return remote(emb.at[to, rows_of(c)], landing(c, n), emb_s.at[c, d], emb_r.at[c, d], (w, to))

    def packed_rows(g):
        return pl.ds(OFFSETS[g], CAPS[g])

    def data_copy(g, k):
        return remote(
            stage.at[k, packed_rows(g)], arrived_ref.at[w, packed_rows(g)],
            data_s.at[g, k], data_r.at[g, k], (wide_peer(k), n),
        )

    def tag_copy(g, k):
        return remote(tag_out.at[k, g], tags_ref.at[w, g], tag_s.at[g, k], tag_r.at[g, k], (wide_peer(k), n))

    def table_copy(d):
        to = narrow_peer(d)
        return remote(table.at[to], table_in.at[n], table_s.at[d], table_r.at[d], (w, to))

    def final_copy(k):
        to = wide_peer(k)
        return remote(final.at[to], final_in.at[w], final_s.at[k], final_r.at[k], (to, n))

    def own_data(g):
        return pltpu.make_async_copy(
            stage.at[SELF, packed_rows(g)], arrived_ref.at[w, packed_rows(g)], own_sem.at[g]
        )

    def own_tag(g):
        return pltpu.make_async_copy(tag_out.at[SELF, g], tags_ref.at[w, g], own_tag_sem.at[g])

    loads = [
        pltpu.make_async_copy(src, dst, load_sem.at[i])
        for i, (src, dst) in enumerate(((feats_hbm, feats), (w1_hbm, w1), (w2_hbm, w2), (w3_hbm, w3)))
    ]
    for load in loads:
        load.start()

    barrier = pltpu.get_barrier_semaphore()

    def greet_wide(i):
        pl.semaphore_signal(barrier, inc=1, device_id=(wide_peer(peer_step(i)), n), device_id_type=MESH)

    def greet_narrow(d):
        pl.semaphore_signal(barrier, inc=1, device_id=(w, narrow_peer(d)), device_id_type=MESH)

    loop(1, NARROW, greet_narrow)
    loop(0, WIDE - 1, greet_wide)

    slot_level = iota((SLOTS, SLOTS), 0)
    cluster_level = iota((SLOTS, SLOTS), 1).astype(F32)
    holder = jnp.sum(jnp.where(slots_ref[...] == slot_level, cluster_level, 0.0), axis=1, keepdims=True)
    owner_of[...] = jnp.broadcast_to(holder, (SLOTS, 128)).astype(jnp.int32)
    place = (iota((SLOTS, 128), 0) % CL_DEV * MOST).astype(F32)
    levels[...] = place
    ranks[...] = jnp.zeros_like(ranks)
    dest_carry[...] = jnp.zeros_like(dest_carry)
    ids_all[n] = ids_ref[...]
    q_wide[w] = query_ref[...]

    def tower(c):
        x = feats[rows_of(c), :]
        first = silu(jnp.dot(x, w1[...], preferred_element_type=F32)).astype(BF16)
        second = silu(jnp.dot(first, w2[...], preferred_element_type=F32)).astype(BF16)
        raw = jnp.dot(second, w3[...], preferred_element_type=F32)
        scale = lax.rsqrt(jnp.mean(raw * raw, axis=1, keepdims=True) + 1e-06)
        embedding = (raw * scale * gain_ref[...]).astype(BF16)
        for j in range(NARROW):
            emb[j, rows_of(c), :] = embedding[:, j * PIECE : (j + 1) * PIECE]
        start = pl.multiple_of(NARROW * STARTS[c] + n * SIZES[c], 128)
        rhs[pl.ds(start, SIZES[c]), 0:128] = emb[n, rows_of(c), :]
    def send_rows(c):
        loop(1, NARROW, lambda d: emb_copy(c, d).start())

    def place_rows():
        loop(1, NARROW, lambda d: ids_copy(d).wait_recv())
        upto = iota((128, 256), 0) <= iota((128, 256), 1)
        sums = upto.astype(F32).astype(BF16)

        def source(m):
            for c in range(CHUNKS):
                for part in range(SIZES[c] // 128):
                    k = STARTS[c] // 128 + part
                    q = NARROW * STARTS[c] // 128 + m * (SIZES[c] // 128) + part
                    row = ids_all[m, k : k + 1, :]
                    named = owner_of[...] == row
                    onehot = jnp.where(named, 1.0, 0.0)
                    counts = jnp.dot(onehot.astype(BF16), sums, preferred_element_type=F32)
                    where = jnp.where(named, counts[:, :128] + levels[...], 0.0)
                    ranks[pl.ds(q, 1), :] = jnp.sum(where, axis=0, keepdims=True)
                    levels[...] += counts[:, 128:]
                    owned = jnp.sum(onehot.reshape(WIDE, CL_DEV, 128), axis=1)
                    ordered = jnp.dot(owned.astype(BF16), sums, preferred_element_type=F32)
                    dest[q] = jnp.where(owned > 0.0, ordered[:, :128] + dest_carry[c] - 1.0, -1.0)
                    dest_carry[c] += ordered[:, 128:]

        loop(0, NARROW, source)

        before = jnp.zeros((WIDE, 128), F32)
        for c in range(CHUNKS):
            shift = before - float(CAPS[c])
            first_block = NARROW * STARTS[c] // 128

            def beyond(i):
                q = first_block + i
                spot = dest[q]
                dest_over[q] = jnp.where(spot >= float(CAPS[c]), spot + shift, -1.0)

            loop(0, NARROW * SIZES[c] // 128, beyond)
            before = before + jnp.maximum(dest_carry[c] - float(CAPS[c]), 0.0)
        most = jnp.max(before, axis=0, keepdims=True)
        spill[...] = jnp.broadcast_to(jnp.where(most > float(CAPS[CHUNKS]), 1.0, 0.0), spill.shape)

        turned = jnp.transpose(ranks[...])
        left = iota((128, 128), 1) < 64
        for q in range(BLOCKS):
            column = jnp.broadcast_to(turned[:, q : q + 1], (128, 128))
            high = jnp.floor(column * (1.0 / 32.0)) * 32.0
            rhs[q * 128 : (q + 1) * 128, 128:256] = jnp.where(left, high, column - high).astype(BF16)

    def spread_queries():
        loop(0, WIDE - 1, lambda i: q_wide_copy(peer_step(i)).wait_recv())
        at = iota((4 * WIDE, 8 * WIDE), 0)
        pick = iota((4 * WIDE, 8 * WIDE), 1) == at // 4 * 8 + at % 4
        spread = q_wide[...].reshape(8 * WIDE, PIECE).astype(BF16)
        q_mine[...] = jnp.dot(pick.astype(F32).astype(BF16), spread, preferred_element_type=F32).astype(BF16)
        q_all[n] = q_mine[...]
        loop(1, NARROW, lambda d: q_narrow_copy(d).start())

    def write_tag(k, g, tag, cap):
        tag = tag + pltpu.roll(tag, 64, 1)
        for half in range(2):
            size = min(cap - 128 * half, 128)
            if size > 0:
                eye = iota((size, 128), 0) == iota((size, 128), 1)
                line = jnp.sum(jnp.where(eye, tag[128 * half : 128 * half + size], 0.0), axis=0, keepdims=True)
            else:
                line = spill[0:1, :]
            tag_out[k, g, half : half + 1, :] = line

    def send_group(k, g):
        @pl.when(k != SELF)
        def _():
            data_copy(g, k).start()
            tag_copy(g, k).start()

        @pl.when(k == SELF)
        def _():
            own_data(g).start()
            own_tag(g).start()

    def pack(c):
        loop(1, NARROW, lambda d: emb_copy(c, d).wait_recv())
        low_block, blocks = NARROW * STARTS[c] // 128, NARROW * SIZES[c] // 128
        cap, over = CAPS[c], CAPS[CHUNKS]
        both = cap + over
        spot = iota((cap, 128), 0).astype(F32)
        spot_over = iota((over, 128), 0).astype(F32)

        def to_owners(i):
            lines = []
            for j in range(BATCH):
                to = wide_peer(BATCH * i + j)
                for spots, level in ((dest, spot), (dest_over, spot_over)):
                    parts = []
                    for q in range(blocks):
                        row = spots[low_block + q, pl.ds(to, 1), :]
                        parts.append(jnp.where(level == row, 1.0, 0.0).astype(BF16))
                    lines.append(jnp.concatenate(parts, axis=1))
            onehot = jnp.concatenate(lines, axis=0)
            source = rhs[low_block * 128 : (low_block + blocks) * 128, :]
            packed = jnp.dot(onehot, source, preferred_element_type=F32)
            for j in range(BATCH):
                k = BATCH * i + j
                main = packed[both * j : both * j + cap]
                stage[k, packed_rows(c), :] = main[:, :128].astype(BF16)
                write_tag(k, c, main[:, 128:], cap)
                send_group(k, c)
                rest = packed[both * j + cap : both * (j + 1)]
                if c > 0:
                    rest = rest + over_sum[k]
                if c < CHUNKS - 1:
                    over_sum[k] = rest
                else:
                    stage[k, packed_rows(CHUNKS), :] = rest[:, :128].astype(BF16)
                    write_tag(k, CHUNKS, rest[:, 128:], over)
                    send_group(k, CHUNKS)

        loop(0, WIDE // BATCH, to_owners)

    def local_best():
        loop(1, NARROW, lambda d: q_narrow_copy(d).wait_recv())
        score = jnp.zeros((4 * WIDE, ROWS), F32)
        for j in range(NARROW):
            score += lax.dot_general(q_all[j], emb[j], NT, preferred_element_type=F32)
        ids_f = ids_ref[...].astype(F32)
        id_row = jnp.concatenate([ids_f[k : k + 1, :] for k in range(8)], axis=1)
        key_row = id_row * float(ROWS) + iota((1, ROWS), 1).astype(F32)
        eye = iota((128, 128), 0) == iota((128, 128), 1)
        order = iota((128, ROWS), 1).astype(F32)
        for k in range(8):
            key = jnp.sum(jnp.where(eye, key_row[:, k * 128 : (k + 1) * 128], 0.0), axis=1, keepdims=True)
            position = jnp.sum(jnp.where(key_row < key, 1.0, 0.0), axis=1, keepdims=True)
            perm[k * 128 : (k + 1) * 128, :] = jnp.where(order == position, 1.0, 0.0).astype(BF16)
        high = score.astype(BF16)
        low = (score - high.astype(F32)).astype(BF16)
        id_high = jnp.floor(id_row * (1.0 / 32.0)) * 32.0
        line = iota((16, ROWS), 0)
        extra = jnp.where(line == 0, id_high, jnp.where(line == 1, id_row - id_high, 0.0)).astype(BF16)
        arranged = jnp.dot(jnp.concatenate([high, low, extra], axis=0), perm[...], preferred_element_type=F32)
        top = arranged[0:64] + arranged[64:128]
        seg = jnp.broadcast_to(arranged[128:129] + arranged[129:130], (8, ROWS))
        lane = iota((8, ROWS), 1)
        for step in (1, 2, 4, 8, 16):
            same = (pltpu.roll(seg, step, 1) == seg) & (lane >= step)
            gate = jnp.where(same, 0.0, -jnp.inf)[0:1]
            top = jnp.maximum(top, pltpu.roll(top, step, 1) + gate)
        closing = (pltpu.roll(seg, ROWS - 1, 1) != seg) | (lane == ROWS - 1)
        end_id = jnp.where(closing, seg, -1.0)[0:1]
        for k in range(ROWS // 128):
            match = owner_of[...].astype(F32) == end_id[:, k * 128 : (k + 1) * 128]
            ends[:, k * 128 : (k + 1) * 128] = jnp.where(match, 1.0, 0.0).astype(BF16)
        high = top.astype(BF16)
        low = (top - high.astype(F32)).astype(BF16)
        ones = jnp.ones((16, ROWS), BF16)
        found = lax.dot_general(jnp.concatenate([high, low, ones], axis=0), ends[...], NT, preferred_element_type=F32)
        by_slot = jnp.where(found[128:129] > 0.0, found[0:64] + found[64:128], -jnp.inf)
        for j in range(NARROW):
            table[j] = by_slot[8 * j : 8 * j + 8]
        table_in[n] = table[n]
        loop(1, NARROW, lambda d: table_copy(d).start())

    def merge_narrow():
        loop(1, NARROW, lambda d: table_copy(d).wait_recv())
        merged = jnp.max(table_in[...], axis=0)
        for o in range(WIDE):
            group = merged[:, o // 4 * 128 : o // 4 * 128 + 128]
            final[o] = pltpu.roll(group, (128 - 32 * (o % 4)) % 128, 1) if o % 4 else group
        final_in[w] = final[w]
        loop(0, WIDE - 1, lambda i: final_copy(peer_step(i)).start())

    def merge_wide():
        loop(0, WIDE - 1, lambda i: final_copy(peer_step(i)).wait_recv())
        best_ref[...] = jnp.max(final_in[...], axis=0)

    for load in loads:
        load.wait()
    tower(0)
    pl.semaphore_wait(barrier, NARROW - 1 + WIDE - 1)
    loop(1, NARROW, lambda d: ids_copy(d).start())
    send_rows(0)
    loop(0, WIDE - 1, lambda i: q_wide_copy(peer_step(i)).start())
    tower(1)
    send_rows(1)
    place_rows()
    pack(0)
    tower(2)
    send_rows(2)
    spread_queries()
    tower(3)
    send_rows(3)
    pack(1)
    local_best()
    pack(2)
    merge_narrow()
    pack(3)
    merge_wide()

    def settle_wide(i):
        k = peer_step(i)
        q_wide_copy(k).wait_send()
        final_copy(k).wait_send()

    def settle_narrow(d):
        ids_copy(d).wait_send()
        q_narrow_copy(d).wait_send()
        table_copy(d).wait_send()

    loop(0, WIDE - 1, settle_wide)
    loop(1, NARROW, settle_narrow)

    for c in range(CHUNKS):
        loop(1, NARROW, lambda d: emb_copy(c, d).wait_send())

    for g in range(GROUPS):

        def settle_group(i):
            data_copy(g, peer_step(i)).wait()
            tag_copy(g, peer_step(i)).wait()

        loop(0, WIDE - 1, settle_group)
        own_data(g).wait()
        own_tag(g).wait()


def run_exchange(features, w_first, w_second, w_third, gain, ids, slots, queries):
    vmem = pl.BlockSpec(memory_space=pltpu.VMEM)
    anywhere = pl.BlockSpec(memory_space=pl.ANY)
    dma = pltpu.SemaphoreType.DMA
    return pl.pallas_call(
        exchange,
        out_shape=(
            jax.ShapeDtypeStruct((WIDE, TOTAL, PIECE), BF16),
            jax.ShapeDtypeStruct((WIDE, GROUPS, 2, 128), F32),
            jax.ShapeDtypeStruct((8, 128), F32),
        ),
        in_specs=[anywhere] * 4 + [vmem] * 4,
        out_specs=(anywhere, anywhere, vmem),
        scratch_shapes=[
            pltpu.VMEM((ROWS, 1024), BF16),
            pltpu.VMEM((1024, 1024), BF16),
            pltpu.VMEM((1024, 1024), BF16),
            pltpu.VMEM((1024, 1024), BF16),
            pltpu.VMEM((NARROW, ROWS, PIECE), BF16),
            pltpu.VMEM((NARROW * ROWS, 256), BF16),
            pltpu.VMEM((WIDE, TOTAL, PIECE), BF16),
            pltpu.VMEM((WIDE, GROUPS, 2, 128), F32),
            pltpu.VMEM((NARROW, 8, 128), jnp.int32),
            pltpu.VMEM((SLOTS, 128), jnp.int32),
            pltpu.VMEM((SLOTS, 128), F32),
            pltpu.VMEM((128, 128), F32),
            pltpu.VMEM((BLOCKS, WIDE, 128), F32),
            pltpu.VMEM((BLOCKS, WIDE, 128), F32),
            pltpu.VMEM((CHUNKS, WIDE, 128), F32),
            pltpu.VMEM((8, 128), F32),
            pltpu.VMEM((WIDE, CAPS[CHUNKS], 256), F32),
            pltpu.VMEM((WIDE, 8, PIECE), F32),
            pltpu.VMEM((4 * WIDE, PIECE), BF16),
            pltpu.VMEM((NARROW, 4 * WIDE, PIECE), BF16),
            pltpu.VMEM((ROWS, ROWS), BF16),
            pltpu.VMEM((SLOTS, ROWS), BF16),
            pltpu.VMEM((NARROW, 8, SLOTS), F32),
            pltpu.VMEM((NARROW, 8, SLOTS), F32),
            pltpu.VMEM((WIDE, 8, 128), F32),
            pltpu.VMEM((WIDE, 8, 128), F32),
            dma((4,)),
            dma((NARROW,)), dma((NARROW,)),
            dma((WIDE,)), dma((WIDE,)),
            dma((NARROW,)), dma((NARROW,)),
            dma((CHUNKS, NARROW)), dma((CHUNKS, NARROW)),
            dma((GROUPS, WIDE)), dma((GROUPS, WIDE)),
            dma((GROUPS, WIDE)), dma((GROUPS, WIDE)),
            dma((NARROW,)), dma((NARROW,)),
            dma((WIDE,)), dma((WIDE,)),
            dma((GROUPS,)), dma((GROUPS,)),
        ],
        compiler_params=pltpu.CompilerParams(
            collective_id=0, has_side_effects=True, vmem_limit_bytes=56 * 2**20
        ),
        name="exchange",
    )(features, w_first, w_second, w_third, gain, ids, slots, queries)


def unpack(arrived_ref, tags_ref, slab_ref):
    spot = iota((CL_DEV * MOST, 1), 0).astype(F32) + 1.0
    parts = []
    for g in range(GROUPS):
        for half in range(2):
            size = min(CAPS[g] - 128 * half, 128)
            if size > 0:
                parts.append(tags_ref[0, g, half : half + 1, :size])
    row = jnp.concatenate(parts, axis=1)
    onehot = jnp.where(spot == row, 1.0, 0.0).astype(BF16)
    slab_ref[0] = jnp.dot(onehot, arrived_ref[0], preferred_element_type=F32).astype(BF16)


def run_unpack(arrived, tags):
    return pl.pallas_call(
        unpack,
        grid=(WIDE,),
        out_shape=jax.ShapeDtypeStruct((WIDE, CL_DEV * MOST, PIECE), BF16),
        in_specs=[
            pl.BlockSpec((1, TOTAL, PIECE), lambda b: (b, 0, 0)),
            pl.BlockSpec((1, GROUPS, 2, 128), lambda b: (b, 0, 0, 0)),
        ],
        out_specs=pl.BlockSpec((1, CL_DEV * MOST, PIECE), lambda b: (b, 0, 0)),
        compiler_params=pltpu.CompilerParams(vmem_limit_bytes=32 * 2**20),
        name="unpack",
    )(arrived, tags)


def pass_on(in_ref, out_ref):
    out_ref[...] = in_ref[...]


def run_pass_on(slab):
    block = pl.BlockSpec((1, CL_DEV * MOST, PIECE), lambda b: (b, 0, 0))
    return pl.pallas_call(
        pass_on,
        grid=(WIDE,),
        out_shape=jax.ShapeDtypeStruct(slab.shape, slab.dtype),
        in_specs=[block],
        out_specs=block,
        name="pass_on",
    )(slab)


def slot_table(id_list, cluster_slots, total):
    levels = jnp.arange(total, dtype=jnp.int32)
    onehot = (id_list[:, None] == levels[None, :]).astype(jnp.bfloat16)
    high_part = (cluster_slots // 64).astype(jnp.bfloat16)
    low_part = (cluster_slots % 64).astype(jnp.bfloat16)
    slot_value = 64.0 * jnp.dot(onehot, high_part, preferred_element_type=jnp.float32) + jnp.dot(
        onehot, low_part, preferred_element_type=jnp.float32
    )
    return (onehot, slot_value.astype(jnp.int32))


def cluster_ranks(onehot):
    count, total = onehot.shape
    block = math.gcd(count, 256)
    number = count // block
    stacked = onehot.reshape(number, block, total)
    inner = jnp.arange(block, dtype=jnp.int32)
    lower = (inner[:, None] >= inner[None, :]).astype(jnp.bfloat16)
    inside = jnp.einsum("rs,bsc->brc", lower, stacked, preferred_element_type=jnp.float32)
    block_sums = inside[:, -1, :]
    outer = jnp.arange(number, dtype=jnp.int32)
    before = (outer[:, None] > outer[None, :]).astype(jnp.float32)
    earlier = jnp.dot(
        before, block_sums, precision=lax.Precision.HIGHEST, preferred_element_type=jnp.float32
    )
    position = jnp.sum(stacked * (inside - 1.0 + earlier[:, None, :]), axis=2)
    return (position.reshape(count).astype(jnp.int32), jnp.sum(block_sums, axis=0))


def padded_slab(features, cluster_ids, cluster_slots, w_first, w_second, w_third, emb_gain):
    first = jax.nn.silu(jnp.dot(features, w_first, preferred_element_type=F32)).astype(BF16)
    second = jax.nn.silu(jnp.dot(first, w_second, preferred_element_type=F32)).astype(BF16)
    raw = jnp.dot(second, w_third, preferred_element_type=F32)
    scale = lax.rsqrt(jnp.mean(raw * raw, axis=1, keepdims=True) + 1e-06)
    embedding = (raw * scale * emb_gain).astype(BF16)
    block_ids = lax.all_gather(cluster_ids[:, 0], "narrow", axis=0, tiled=True)
    block_rows = block_ids.shape[0]
    onehot, slot_of = slot_table(block_ids, cluster_slots, SLOTS)
    positions, _ = cluster_ranks(onehot)
    flat_slot = slot_of * MOST + positions
    sliced = lax.all_to_all(embedding, "narrow", split_axis=1, concat_axis=0, tiled=True)
    source = (
        jnp.full((SLOTS * MOST,), block_rows, jnp.int32)
        .at[flat_slot]
        .set(jnp.arange(block_rows, dtype=jnp.int32))
    )
    padded = jnp.concatenate([sliced, jnp.zeros((1, PIECE), BF16)], axis=0)
    outgoing = jnp.take(padded, source, axis=0).reshape(WIDE, CL_DEV * MOST, PIECE)
    return run_pass_on(lax.all_to_all(outgoing, "wide", split_axis=0, concat_axis=0, tiled=True))


def shards(features, cluster_ids, cluster_slots, w_first, w_second, w_third, emb_gain, queries):
    ids = cluster_ids.reshape(8, 128)
    query = jnp.pad(queries.astype(F32), ((0, 4), (0, 0)))
    arrived, tags, best = run_exchange(
        features, w_first, w_second, w_third, emb_gain.reshape(1, 1024), ids, cluster_slots.reshape(1, SLOTS), query
    )
    fits = jnp.max(tags[:, CHUNKS, 1, 0]) == 0.0
    slab = lax.cond(
        fits,
        lambda: run_unpack(arrived, tags),
        lambda: padded_slab(features, cluster_ids, cluster_slots, w_first, w_second, w_third, emb_gain),
    )
    return (best[:, :CL_DEV], slab.reshape(WIDE, CL_DEV, MOST, PIECE))


def solution(mesh):
    placed = (
        P(("wide", "narrow"), None),
        P(("wide", "narrow"), None),
        P(),
        P(),
        P(),
        P(),
        P(),
        P("wide", "narrow"),
    )
    return jax.shard_map(
        shards,
        mesh=mesh,
        in_specs=placed,
        out_specs=(P("narrow", "wide"), P(None, "wide", None, "narrow")),
        check_vma=False,
    )
```

time: 103 us -> 94.9 us (0.921)
  local copies, waits for them, and re-layouts: 5.74 us -> 0.61 us
  Pallas kernels: 93.5 us -> 90.6 us
    unnamed x12 -> x11, local copies, waits for them, and re-layouts: 5.74 us -> 0.61 us
    pallas_call x1, Pallas kernels: 78 us -> 75.9 us  [run_exchange(): pl.pallas_call(exchange, out_shape=(jax.ShapeDtypeStruct((WIDE, TOTAL, PI...]
where the time goes in v2:
time: 94.9 us; the launch traced here: 94.4 us
  Pallas kernels  90.6 us (95%)
  other arithmetic  1.89 us (2%)
  between operations  1.34 us (1%)
    pallas_call x1, Pallas kernels, run_exchange(): pl.pallas_call(exchange, out_shape=(jax.ShapeDtypeStruct((WIDE, TOTAL, PI...  75.9 us
    pallas_call x1, Pallas kernels, run_unpack(): pl.pallas_call(unpack, grid=(WIDE,), out_shape=jax.ShapeDtypeStruct((WIDE...  14.7 us

profile of v2, /device:TPU:1, one launch (start us, length us, event | category | flops | bytes accessed | tf_op | source)
XLA Modules:
  0.0 94.4 jit_solution(11033840904931242642)
XLA Ops:
  0.6 1.3 %pad_convert_fusion.query_ref = f32[8,128]{1,0:T(8,128)} fusion(bf16[4,128]{1,0:T(4,128)(2,1)} %param.17), kind=kLoop, calls=%fused_computation.46 | loop fusion | flops 1024 | bytes 5120 | tf_op jit(solution)/shard_map/jit(_pad)/pad | solution.py:546
  1.9 0.0 copy-start
  1.9 0.0 copy-start.1
  1.9 0.0 copy-start.2
  1.9 0.0 copy-start.3
  1.9 75.9 %exchange.1 = (bf16[16,752,128]{2,1,0:T(8,128)(2,1)}, f32[16,5,2,128]{3,2,1,0:T(2,128)S(1)}, f32[8,128]{1,0:T(8,128)}) custom-call(bf16[1024,1024]{1,0:T(8,128)(2,1)} %feats_hbm.1, bf16[1024,1024]{1,0:T(8,128)(2,1)} %w1_hbm.1, bf16[1024,1024]{1,0:T(8,128)(2,1)} %w2_hbm.1, bf16[1024,1024]{1,0:T(8,128)(2,1)} %w3_hbm.1, f32[1,1024]{1,0:T(1,128)} %bitcast.42, ...), custom_call_target="tpu_custom_call" | custom-call | tf_op jit(solution)/shard_map/exchange/pallas_call | solution.py:395
  77.8 0.6 slice_reduce_fusion
  79.1 0.0 copy-done
  79.1 0.0 copy-done.1
  79.1 0.0 copy-done.2
  79.1 0.0 copy-done.3
  79.1 0.0 copy-start.4
  79.2 14.7 %conditional.1 = (bf16[16,32,32,128]{3,2,1,0:T(8,128)(2,1)}) conditional(s32[]{:T(128)} %convert_element_type.39, (s32[1024,1]{0,1:T(1,128)S(1)}, s32[512]{0:T(512)S(1)}, bf16[1024,1024]{1,0:T(8,128)(2,1)S(1)}, bf16[1024,1024]{1,0:T(8,128)(2,1)}, bf16[1024,1024]{1,0:T(8,128)(2,1)}, /*index=5*/bf16[1024,1024]{1,0:T(8,128)(2,1)}, ...), branch_computations={%region_1.5_spmd, %region_5.6_spmd} | conditional | flops 8673079296 | bytes 102107448 | solution.py:551
  79.2 14.7 %unpack.1 = bf16[16,1024,128]{2,1,0:T(8,128)(2,1)} custom-call(bf16[16,752,128]{2,1,0:T(8,128)(2,1)} %get-tuple-element.29.arrived_ref, f32[16,5,2,128]{3,2,1,0:T(2,128)S(1)} %get-tuple-element.30.tags_ref), custom_call_target="tpu_custom_call" | custom-call | tf_op jit(solution)/shard_map/cond/branch_1_fun/unpack/pallas_call | solution.py:463
  93.8 0.0 copy-done.4
  93.8 0.6 copy.20
Async XLA Ops:
  1.9 77.2 %copy-start = (bf16[1024,1024]{1,0:T(8,128)(2,1)S(1)}, bf16[1024,1024]{1,0:T(8,128)(2,1)}, u32[]{:S(2)}) copy-start(bf16[1024,1024]{1,0:T(8,128)(2,1)} %feats_hbm.1) | copy-start | bytes 6291460
  1.9 77.2 %copy-start.1 = (f32[1024]{0:T(1024)S(1)}, f32[1024]{0:T(1024)}, u32[]{:S(2)}) copy-start(f32[1024]{0:T(1024)} %param.16) | copy-start | bytes 12292
  1.9 77.2 %copy-start.2 = (s32[1024,1]{0,1:T(1,128)S(1)}, s32[1024,1]{0,1:T(1,128)}, u32[]{:S(2)}) copy-start(s32[1024,1]{0,1:T(1,128)} %param.11) | copy-start | bytes 12292
  1.9 77.2 %copy-start.3 = (s32[512]{0:T(512)S(1)}, s32[512]{0:T(512)}, u32[]{:S(2)}) copy-start(s32[512]{0:T(512)} %param.12) | copy-start | bytes 6148
  79.1 14.7 %copy-start.4 = (f32[8,128]{1,0:T(8,128)S(1)}, f32[8,128]{1,0:T(8,128)}, u32[]{:S(2)}) copy-start(f32[8,128]{1,0:T(8,128)} %get-tuple-element.36) | copy-start | bytes 12292

commit v3 on v2

--- a/solution.py
+++ b/solution.py
@@ -16,13 +16,13 @@
 ROWS = 1024
 PIECE = 128
 SLOTS = 512
-SIZES = (256, 256, 256, 256)
-CAPS = (176, 176, 176, 176, 48)
-CHUNKS = len(SIZES)
+CHUNKS = 4
+CHUNK = ROWS // CHUNKS
+PARTS = CHUNK // 128
+CAP = 176
+OVER = 48
 GROUPS = CHUNKS + 1
-STARTS = tuple(sum(SIZES[:c]) for c in range(CHUNKS))
-OFFSETS = tuple(sum(CAPS[:g]) for g in range(GROUPS))
-TOTAL = sum(CAPS)
+TOTAL = CHUNKS * CAP + OVER
 BLOCKS = NARROW * ROWS // 128
 SELF = 2
 BATCH = 4
@@ -55,9 +55,9 @@
 def exchange(
     feats_hbm, w1_hbm, w2_hbm, w3_hbm, gain_ref, ids_ref, slots_ref, query_ref,
     arrived_ref, tags_ref, best_ref,
-    feats, w1, w2, w3, emb, rhs, stage, tag_out, ids_all, owner_of, levels, ranks, dest, dest_over, dest_carry, spill, over_sum,
+    feats, w1, w2, w3, emb, rhs, stage, tag_out, notes, notes_all, rank_all, owner_of, levels, dest, dest_over, spill, over_sum,
     q_wide, q_mine, q_all, perm, ends, table, table_in, final, final_in,
-    load_sem, ids_s, ids_r, qw_s, qw_r, qn_s, qn_r, emb_s, emb_r, data_s, data_r, tag_s, tag_r,
+    load_sem, notes_s, notes_r, qw_s, qw_r, qn_s, qn_r, emb_s, emb_r, data_s, data_r, tag_s, tag_r,
     table_s, table_r, final_s, final_r, own_sem, own_tag_sem,
 ):
     w = lax.axis_index("wide")
@@ -76,8 +76,8 @@
             src_ref=src, dst_ref=dst, send_sem=send, recv_sem=recv, device_id=device, device_id_type=MESH
         )
 
-    def ids_copy(d):
-        return remote(ids_ref, ids_all.at[n], ids_s.at[d], ids_r.at[d], (w, narrow_peer(d)))
+    def notes_copy(d):
+        return remote(notes, notes_all.at[n], notes_s.at[d], notes_r.at[d], (w, narrow_peer(d)))
 
     def q_wide_copy(k):
         return remote(query_ref, q_wide.at[w], qw_s.at[k], qw_r.at[k], (wide_peer(k), n))
@@ -86,22 +86,25 @@
         return remote(q_mine, q_all.at[n], qn_s.at[d], qn_r.at[d], (w, narrow_peer(d)))
 
     def rows_of(c):
-        return pl.ds(STARTS[c], SIZES[c])
+        return pl.ds(pl.multiple_of(c * CHUNK, CHUNK), CHUNK)
 
     def landing(c, m):
-        start = NARROW * STARTS[c] + m * SIZES[c]
-        return rhs.at[pl.ds(pl.multiple_of(start, 128), SIZES[c]), pl.ds(0, 128)]
+        return pl.ds(pl.multiple_of((NARROW * c + m) * CHUNK, CHUNK), CHUNK)
 
     def emb_copy(c, d):
         to = narrow_peer(d)
-        return remote(emb.at[to, rows_of(c)], landing(c, n), emb_s.at[c, d], emb_r.at[c, d], (w, to))
-
-    def packed_rows(g):
-        return pl.ds(OFFSETS[g], CAPS[g])
-
-    def data_copy(g, k):
         return remote(
-            stage.at[k, packed_rows(g)], arrived_ref.at[w, packed_rows(g)],
+            emb.at[to, rows_of(c)], rhs.at[landing(c, n), pl.ds(0, 128)],
+            emb_s.at[c, d], emb_r.at[c, d], (w, to),
+        )
+
+    def packed_rows(g, last=False):
+        return pl.ds(pl.multiple_of(g * CAP, 16), OVER if last else CAP)
+
+    def data_copy(g, k, last=False):
+        rows = packed_rows(g, last)
+        return remote(
+            stage.at[k, rows], arrived_ref.at[w, rows],
             data_s.at[g, k], data_r.at[g, k], (wide_peer(k), n),
         )
 
@@ -116,20 +119,28 @@
         to = wide_peer(k)
         return remote(final.at[to], final_in.at[w], final_s.at[k], final_r.at[k], (to, n))
 
-    def own_data(g):
-        return pltpu.make_async_copy(
-            stage.at[SELF, packed_rows(g)], arrived_ref.at[w, packed_rows(g)], own_sem.at[g]
-        )
+    def own_data(g, last=False):
+        rows = packed_rows(g, last)
+        return pltpu.make_async_copy(stage.at[SELF, rows], arrived_ref.at[w, rows], own_sem.at[g])
 
     def own_tag(g):
         return pltpu.make_async_copy(tag_out.at[SELF, g], tags_ref.at[w, g], own_tag_sem.at[g])
 
-    loads = [
-        pltpu.make_async_copy(src, dst, load_sem.at[i])
-        for i, (src, dst) in enumerate(((feats_hbm, feats), (w1_hbm, w1), (w2_hbm, w2), (w3_hbm, w3)))
+    def load(src, dst, part, i):
+        rows = pl.ds(part * 256, 256)
+        return pltpu.make_async_copy(src.at[rows], dst.at[rows], load_sem.at[i, part])
+
+    feat_loads = [load(feats_hbm, feats, part, 0) for part in range(4)]
+    weight_loads = [
+        [load(src, dst, part, i + 1) for part in range(4)]
+        for i, (src, dst) in enumerate(((w1_hbm, w1), (w2_hbm, w2), (w3_hbm, w3)))
     ]
-    for load in loads:
-        load.start()
+    feat_loads[0].start()
+    for group in weight_loads:
+        for copy in group:
+            copy.start()
+    for copy in feat_loads[1:]:
+        copy.start()
 
     barrier = pltpu.get_barrier_semaphore()
 
@@ -146,12 +157,31 @@
     cluster_level = iota((SLOTS, SLOTS), 1).astype(F32)
     holder = jnp.sum(jnp.where(slots_ref[...] == slot_level, cluster_level, 0.0), axis=1, keepdims=True)
     owner_of[...] = jnp.broadcast_to(holder, (SLOTS, 128)).astype(jnp.int32)
-    place = (iota((SLOTS, 128), 0) % CL_DEV * MOST).astype(F32)
-    levels[...] = place
-    ranks[...] = jnp.zeros_like(ranks)
-    dest_carry[...] = jnp.zeros_like(dest_carry)
-    ids_all[n] = ids_ref[...]
     q_wide[w] = query_ref[...]
+    sums = (iota((128, 256), 0) <= iota((128, 256), 1)).astype(F32).astype(BF16)
+
+    def note_rows():
+        slot = iota((SLOTS, 128), 0)
+        place = (slot % CL_DEV * MOST).astype(F32)
+        level = slot.astype(F32)
+        levels[...] = place
+
+        def note(k):
+            lanes = pl.ds(pl.multiple_of(k * 128, 128), 128)
+            named = owner_of[...] == ids_ref[pl.ds(k, 1), :]
+            onehot = jnp.where(named, 1.0, 0.0).astype(BF16)
+            ends[:, lanes] = onehot
+            counts = jnp.dot(onehot, sums, preferred_element_type=F32)
+            spot = jnp.where(named, counts[:, :128] + levels[...], 0.0)
+            notes[pl.ds(8 + k, 1), :] = jnp.sum(spot, axis=0, keepdims=True)
+            notes[pl.ds(k, 1), :] = jnp.sum(jnp.where(named, level, 0.0), axis=0, keepdims=True)
+            levels[...] += counts[:, 128:]
+
+        loop(0, 8, note)
+        number = (levels[...] - place).reshape(WIDE, CL_DEV, 128)
+        inner = (iota((CL_DEV, 128), 0) == iota((CL_DEV, 128), 1)).astype(F32)
+        notes[16:32, :] = jnp.sum(number * inner[None], axis=1)
+        notes_all[n] = notes[...]
 
     def tower(c):
         x = feats[rows_of(c), :]
@@ -162,56 +192,63 @@
         embedding = (raw * scale * gain_ref[...]).astype(BF16)
         for j in range(NARROW):
             emb[j, rows_of(c), :] = embedding[:, j * PIECE : (j + 1) * PIECE]
-        start = pl.multiple_of(NARROW * STARTS[c] + n * SIZES[c], 128)
-        rhs[pl.ds(start, SIZES[c]), 0:128] = emb[n, rows_of(c), :]
+        rhs[landing(c, n), 0:128] = emb[n, rows_of(c), :]
+
     def send_rows(c):
         loop(1, NARROW, lambda d: emb_copy(c, d).start())
 
     def place_rows():
-        loop(1, NARROW, lambda d: ids_copy(d).wait_recv())
-        upto = iota((128, 256), 0) <= iota((128, 256), 1)
-        sums = upto.astype(F32).astype(BF16)
-
-        def source(m):
-            for c in range(CHUNKS):
-                for part in range(SIZES[c] // 128):
-                    k = STARTS[c] // 128 + part
-                    q = NARROW * STARTS[c] // 128 + m * (SIZES[c] // 128) + part
-                    row = ids_all[m, k : k + 1, :]
-                    named = owner_of[...] == row
-                    onehot = jnp.where(named, 1.0, 0.0)
-                    counts = jnp.dot(onehot.astype(BF16), sums, preferred_element_type=F32)
-                    where = jnp.where(named, counts[:, :128] + levels[...], 0.0)
-                    ranks[pl.ds(q, 1), :] = jnp.sum(where, axis=0, keepdims=True)
-                    levels[...] += counts[:, 128:]
-                    owned = jnp.sum(onehot.reshape(WIDE, CL_DEV, 128), axis=1)
-                    ordered = jnp.dot(owned.astype(BF16), sums, preferred_element_type=F32)
-                    dest[q] = jnp.where(owned > 0.0, ordered[:, :128] + dest_carry[c] - 1.0, -1.0)
-                    dest_carry[c] += ordered[:, 128:]
-
-        loop(0, NARROW, source)
-
-        before = jnp.zeros((WIDE, 128), F32)
-        for c in range(CHUNKS):
-            shift = before - float(CAPS[c])
-            first_block = NARROW * STARTS[c] // 128
-
-            def beyond(i):
-                q = first_block + i
-                spot = dest[q]
-                dest_over[q] = jnp.where(spot >= float(CAPS[c]), spot + shift, -1.0)
-
-            loop(0, NARROW * SIZES[c] // 128, beyond)
-            before = before + jnp.maximum(dest_carry[c] - float(CAPS[c]), 0.0)
+        loop(1, NARROW, lambda d: notes_copy(d).wait_recv())
+        earlier = [jnp.zeros((WIDE, 128), F32)]
+        for m in range(NARROW - 1):
+            earlier.append(earlier[m] + notes_all[m, 16:32, :])
+        earlier = [number.astype(BF16) for number in earlier]
+        inside_level = iota((128, 128), 0).astype(F32)
+        owner_level = iota((WIDE, 128), 0).astype(F32)
+        cap = float(CAP)
+
+        def place_chunk(c, before):
+            held = []
+            for m in range(NARROW):
+                for part in range(PARTS):
+                    k = PARTS * c + part
+                    row = notes_all[m, pl.ds(k, 1), :]
+                    owner = jnp.floor(row * (1.0 / CL_DEV))
+                    held.append(jnp.where(owner_level == owner, 1.0, 0.0))
+                    inside = jnp.where(inside_level == row - owner * CL_DEV, 1.0, 0.0).astype(BF16)
+                    ahead = jnp.dot(earlier[m], inside, preferred_element_type=F32) * held[-1]
+                    rank_all[m, pl.ds(k, 1), :] = notes_all[m, pl.ds(8 + k, 1), :] + jnp.sum(
+                        ahead, axis=0, keepdims=True
+                    )
+            ordered = jnp.dot(jnp.concatenate(held, axis=0).astype(BF16), sums, preferred_element_type=F32)
+            carry = jnp.zeros((WIDE, 128), F32)
+            for q in range(NARROW * PARTS):
+                spot = ordered[WIDE * q : WIDE * (q + 1), :128] + carry - 1.0
+                spot = jnp.where(held[q] > 0.0, spot, -1.0)
+                dest[NARROW * PARTS * c + q] = spot
+                dest_over[NARROW * PARTS * c + q] = jnp.where(spot >= cap, spot - cap + before, -1.0)
+                carry = carry + ordered[WIDE * q : WIDE * (q + 1), 128:]
+            return before + jnp.maximum(carry - cap, 0.0)
+
+        before = lax.fori_loop(0, CHUNKS, place_chunk, jnp.zeros((WIDE, 128), F32))
         most = jnp.max(before, axis=0, keepdims=True)
-        spill[...] = jnp.broadcast_to(jnp.where(most > float(CAPS[CHUNKS]), 1.0, 0.0), spill.shape)
-
-        turned = jnp.transpose(ranks[...])
+        spill[...] = jnp.broadcast_to(jnp.where(most > float(OVER), 1.0, 0.0), spill.shape)
+
+        ranks = rank_all[...].reshape(BLOCKS, 128)
+        turned = jnp.transpose(jnp.concatenate([ranks, jnp.zeros((128 - BLOCKS, 128), F32)], axis=0))
         left = iota((128, 128), 1) < 64
-        for q in range(BLOCKS):
-            column = jnp.broadcast_to(turned[:, q : q + 1], (128, 128))
-            high = jnp.floor(column * (1.0 / 32.0)) * 32.0
-            rhs[q * 128 : (q + 1) * 128, 128:256] = jnp.where(left, high, column - high).astype(BF16)
+
+        def tag_chunk(c):
+            moved = pltpu.roll(turned, (128 - PARTS * c) % 128, 1)
+            for m in range(NARROW):
+                for part in range(PARTS):
+                    at = 8 * m + part
+                    column = jnp.broadcast_to(moved[:, at : at + 1], (128, 128))
+                    high = jnp.floor(column * (1.0 / 32.0)) * 32.0
+                    rows = pl.ds(pl.multiple_of((NARROW * c + m) * CHUNK + part * 128, 128), 128)
+                    rhs[rows, 128:256] = jnp.where(left, high, column - high).astype(BF16)
+
+        loop(0, CHUNKS, tag_chunk)
 
     def spread_queries():
         loop(0, WIDE - 1, lambda i: q_wide_copy(peer_step(i)).wait_recv())
@@ -233,24 +270,23 @@
                 line = spill[0:1, :]
             tag_out[k, g, half : half + 1, :] = line
 
-    def send_group(k, g):
+    def send_group(k, g, last=False):
         @pl.when(k != SELF)
         def _():
-            data_copy(g, k).start()
+            data_copy(g, k, last).start()
             tag_copy(g, k).start()
 
         @pl.when(k == SELF)
         def _():
-            own_data(g).start()
+            own_data(g, last).start()
             own_tag(g).start()
 
     def pack(c):
         loop(1, NARROW, lambda d: emb_copy(c, d).wait_recv())
-        low_block, blocks = NARROW * STARTS[c] // 128, NARROW * SIZES[c] // 128
-        cap, over = CAPS[c], CAPS[CHUNKS]
-        both = cap + over
-        spot = iota((cap, 128), 0).astype(F32)
-        spot_over = iota((over, 128), 0).astype(F32)
+        blocks = NARROW * PARTS
+        both = CAP + OVER
+        spot = iota((CAP, 128), 0).astype(F32)
+        spot_over = iota((OVER, 128), 0).astype(F32)
 
         def to_owners(i):
             lines = []
@@ -259,29 +295,30 @@
                 for spots, level in ((dest, spot), (dest_over, spot_over)):
                     parts = []
                     for q in range(blocks):
-                        row = spots[low_block + q, pl.ds(to, 1), :]
+                        row = spots[blocks * c + q, pl.ds(to, 1), :]
                         parts.append(jnp.where(level == row, 1.0, 0.0).astype(BF16))
                     lines.append(jnp.concatenate(parts, axis=1))
             onehot = jnp.concatenate(lines, axis=0)
-            source = rhs[low_block * 128 : (low_block + blocks) * 128, :]
+            source = rhs[pl.ds(pl.multiple_of(c * (NARROW * CHUNK), NARROW * CHUNK), NARROW * CHUNK), :]
             packed = jnp.dot(onehot, source, preferred_element_type=F32)
             for j in range(BATCH):
                 k = BATCH * i + j
-                main = packed[both * j : both * j + cap]
+                main = packed[both * j : both * j + CAP]
                 stage[k, packed_rows(c), :] = main[:, :128].astype(BF16)
-                write_tag(k, c, main[:, 128:], cap)
+                write_tag(k, c, main[:, 128:], CAP)
                 send_group(k, c)
-                rest = packed[both * j + cap : both * (j + 1)]
-                if c > 0:
-                    rest = rest + over_sum[k]
-                if c < CHUNKS - 1:
-                    over_sum[k] = rest
-                else:
-                    stage[k, packed_rows(CHUNKS), :] = rest[:, :128].astype(BF16)
-                    write_tag(k, CHUNKS, rest[:, 128:], over)
-                    send_group(k, CHUNKS)
+                over_sum[k] += packed[both * j + CAP : both * (j + 1)]
 
         loop(0, WIDE // BATCH, to_owners)
+
+    def pack_over():
+        def to_owner(k):
+            rest = over_sum[k]
+            stage[k, packed_rows(CHUNKS, True), :] = rest[:, :128].astype(BF16)
+            write_tag(k, CHUNKS, rest[:, 128:], OVER)
+            send_group(k, CHUNKS, True)
+
+        loop(0, WIDE, to_owner)
 
     def local_best():
         loop(1, NARROW, lambda d: q_narrow_copy(d).wait_recv())
@@ -338,27 +375,49 @@
         loop(0, WIDE - 1, lambda i: final_copy(peer_step(i)).wait_recv())
         best_ref[...] = jnp.max(final_in[...], axis=0)
 
-    for load in loads:
-        load.wait()
-    tower(0)
-    pl.semaphore_wait(barrier, NARROW - 1 + WIDE - 1)
-    loop(1, NARROW, lambda d: ids_copy(d).start())
-    send_rows(0)
-    loop(0, WIDE - 1, lambda i: q_wide_copy(peer_step(i)).start())
-    tower(1)
-    send_rows(1)
-    place_rows()
-    pack(0)
-    tower(2)
-    send_rows(2)
-    spread_queries()
-    tower(3)
-    send_rows(3)
-    pack(1)
-    local_best()
-    pack(2)
+    over_sum[...] = jnp.zeros_like(over_sum)
+    note_rows()
+    for group in [feat_loads] + weight_loads:
+        for copy in group:
+            copy.wait()
+
+    def turn(t):
+        @pl.when(t < CHUNKS)
+        def _():
+            tower(t)
+
+        @pl.when(t == 0)
+        def _():
+            pl.semaphore_wait(barrier, NARROW - 1 + WIDE - 1)
+            loop(1, NARROW, lambda d: notes_copy(d).start())
+
+        @pl.when(t < CHUNKS)
+        def _():
+            send_rows(t)
+
+        @pl.when(t == 0)
+        def _():
+            loop(0, WIDE - 1, lambda i: q_wide_copy(peer_step(i)).start())
+
+        @pl.when(t == 1)
+        def _():
+            place_rows()
+
+        @pl.when(t == 2)
+        def _():
+            spread_queries()
+
+        @pl.when(t == CHUNKS)
+        def _():
+            local_best()
+
+        @pl.when(t >= 1)
+        def _():
+            pack(t - 1)
+
+    loop(0, CHUNKS + 1, turn)
+    pack_over()
     merge_narrow()
-    pack(3)
     merge_wide()
 
     def settle_wide(i):
@@ -367,25 +426,28 @@
         final_copy(k).wait_send()
 
     def settle_narrow(d):
-        ids_copy(d).wait_send()
+        notes_copy(d).wait_send()
         q_narrow_copy(d).wait_send()
         table_copy(d).wait_send()
 
     loop(0, WIDE - 1, settle_wide)
     loop(1, NARROW, settle_narrow)
 
-    for c in range(CHUNKS):
+    def settle_chunk(c):
         loop(1, NARROW, lambda d: emb_copy(c, d).wait_send())
-
-    for g in range(GROUPS):
-
-        def settle_group(i):
-            data_copy(g, peer_step(i)).wait()
+        settle_group(c, False)
+
+    def settle_group(g, last):
+        def settle(i):
+            data_copy(g, peer_step(i), last).wait()
             tag_copy(g, peer_step(i)).wait()
 
-        loop(0, WIDE - 1, settle_group)
-        own_data(g).wait()
+        loop(0, WIDE - 1, settle)
+        own_data(g, last).wait()
         own_tag(g).wait()
+
+    loop(0, CHUNKS, settle_chunk)
+    settle_group(CHUNKS, True)
 
 
 def run_exchange(features, w_first, w_second, w_third, gain, ids, slots, queries):
@@ -410,15 +472,15 @@
             pltpu.VMEM((NARROW * ROWS, 256), BF16),
             pltpu.VMEM((WIDE, TOTAL, PIECE), BF16),
             pltpu.VMEM((WIDE, GROUPS, 2, 128), F32),
-            pltpu.VMEM((NARROW, 8, 128), jnp.int32),
+            pltpu.VMEM((32, 128), F32),
+            pltpu.VMEM((NARROW, 32, 128), F32),
+            pltpu.VMEM((NARROW, 8, 128), F32),
             pltpu.VMEM((SLOTS, 128), jnp.int32),
             pltpu.VMEM((SLOTS, 128), F32),
-            pltpu.VMEM((128, 128), F32),
             pltpu.VMEM((BLOCKS, WIDE, 128), F32),
             pltpu.VMEM((BLOCKS, WIDE, 128), F32),
-            pltpu.VMEM((CHUNKS, WIDE, 128), F32),
             pltpu.VMEM((8, 128), F32),
-            pltpu.VMEM((WIDE, CAPS[CHUNKS], 256), F32),
+            pltpu.VMEM((WIDE, OVER, 256), F32),
             pltpu.VMEM((WIDE, 8, PIECE), F32),
             pltpu.VMEM((4 * WIDE, PIECE), BF16),
             pltpu.VMEM((NARROW, 4 * WIDE, PIECE), BF16),
@@ -428,7 +490,7 @@
             pltpu.VMEM((NARROW, 8, SLOTS), F32),
             pltpu.VMEM((WIDE, 8, 128), F32),
             pltpu.VMEM((WIDE, 8, 128), F32),
-            dma((4,)),
+            dma((4, 4)),
             dma((NARROW,)), dma((NARROW,)),
             dma((WIDE,)), dma((WIDE,)),
             dma((NARROW,)), dma((NARROW,)),
@@ -451,7 +513,7 @@
     parts = []
     for g in range(GROUPS):
         for half in range(2):
-            size = min(CAPS[g] - 128 * half, 128)
+            size = min((CAP if g < CHUNKS else OVER) - 128 * half, 128)
             if size > 0:
                 parts.append(tags_ref[0, g, half : half + 1, :size])
     row = jnp.concatenate(parts, axis=1)

time: 94.9 us -> 89.1 us (0.939)
  Pallas kernels: 90.6 us -> 84.6 us
    pallas_call x1, Pallas kernels: 75.9 us -> 69.9 us  [run_exchange(): pl.pallas_call(exchange, out_shape=(jax.ShapeDtypeStruct((WIDE, TOTAL, PI...]
where the time goes in v3:
time: 89.1 us; the launch traced here: 88.6 us
  Pallas kernels  84.6 us (95%)
  other arithmetic  1.89 us (2%)
  between operations  1.34 us (2%)
    pallas_call x1, Pallas kernels, run_exchange(): pl.pallas_call(exchange, out_shape=(jax.ShapeDtypeStruct((WIDE, TOTAL, PI...  69.9 us
    pallas_call x1, Pallas kernels, run_unpack(): pl.pallas_call(unpack, grid=(WIDE,), out_shape=jax.ShapeDtypeStruct((WIDE...  14.7 us

profile of v3, /device:TPU:1, one launch (start us, length us, event | category | flops | bytes accessed | tf_op | source)
XLA Modules:
  0.0 88.6 jit_solution(5422412336889173549)
XLA Ops:
  0.6 1.3 %pad_convert_fusion.query_ref = f32[8,128]{1,0:T(8,128)} fusion(bf16[4,128]{1,0:T(4,128)(2,1)} %param.17), kind=kLoop, calls=%fused_computation.46 | loop fusion | flops 1024 | bytes 5120 | tf_op jit(solution)/shard_map/jit(_pad)/pad | solution.py:608
  1.9 0.0 copy-start
  1.9 0.0 copy-start.1
  1.9 0.0 copy-start.2
  1.9 0.0 copy-start.3
  1.9 69.9 %exchange.1 = (bf16[16,752,128]{2,1,0:T(8,128)(2,1)}, f32[16,5,2,128]{3,2,1,0:T(2,128)S(1)}, f32[8,128]{1,0:T(8,128)}) custom-call(bf16[1024,1024]{1,0:T(8,128)(2,1)} %feats_hbm.1, bf16[1024,1024]{1,0:T(8,128)(2,1)} %w1_hbm.1, bf16[1024,1024]{1,0:T(8,128)(2,1)} %w2_hbm.1, bf16[1024,1024]{1,0:T(8,128)(2,1)} %w3_hbm.1, f32[1,1024]{1,0:T(1,128)} %bitcast.42, ...), custom_call_target="tpu_custom_call" | custom-call | tf_op jit(solution)/shard_map/exchange/pallas_call | solution.py:457
  71.8 0.6 slice_reduce_fusion
  73.1 0.0 copy-done
  73.1 0.0 copy-done.1
  73.1 0.0 copy-done.2
  73.1 0.0 copy-done.3
  73.1 0.0 copy-start.4
  73.1 14.9 %conditional.1 = (bf16[16,32,32,128]{3,2,1,0:T(8,128)(2,1)}) conditional(s32[]{:T(128)} %convert_element_type.39, (s32[1024,1]{0,1:T(1,128)S(1)}, s32[512]{0:T(512)S(1)}, bf16[1024,1024]{1,0:T(8,128)(2,1)S(1)}, bf16[1024,1024]{1,0:T(8,128)(2,1)}, bf16[1024,1024]{1,0:T(8,128)(2,1)}, /*index=5*/bf16[1024,1024]{1,0:T(8,128)(2,1)}, ...), branch_computations={%region_1.5_spmd, %region_5.6_spmd} | conditional | flops 8673079296 | bytes 102107448 | solution.py:613
  73.4 14.7 %unpack.1 = bf16[16,1024,128]{2,1,0:T(8,128)(2,1)} custom-call(bf16[16,752,128]{2,1,0:T(8,128)(2,1)} %get-tuple-element.29.arrived_ref, f32[16,5,2,128]{3,2,1,0:T(2,128)S(1)} %get-tuple-element.30.tags_ref), custom_call_target="tpu_custom_call" | custom-call | tf_op jit(solution)/shard_map/cond/branch_1_fun/unpack/pallas_call | solution.py:525
  88.0 0.0 copy-done.4
  88.0 0.6 copy.20
Async XLA Ops:
  1.9 71.2 %copy-start = (bf16[1024,1024]{1,0:T(8,128)(2,1)S(1)}, bf16[1024,1024]{1,0:T(8,128)(2,1)}, u32[]{:S(2)}) copy-start(bf16[1024,1024]{1,0:T(8,128)(2,1)} %feats_hbm.1) | copy-start | bytes 6291460
  1.9 71.2 %copy-start.1 = (f32[1024]{0:T(1024)S(1)}, f32[1024]{0:T(1024)}, u32[]{:S(2)}) copy-start(f32[1024]{0:T(1024)} %param.16) | copy-start | bytes 12292
  1.9 71.2 %copy-start.2 = (s32[1024,1]{0,1:T(1,128)S(1)}, s32[1024,1]{0,1:T(1,128)}, u32[]{:S(2)}) copy-start(s32[1024,1]{0,1:T(1,128)} %param.11) | copy-start | bytes 12292
  1.9 71.2 %copy-start.3 = (s32[512]{0:T(512)S(1)}, s32[512]{0:T(512)}, u32[]{:S(2)}) copy-start(s32[512]{0:T(512)} %param.12) | copy-start | bytes 6148
  73.1 14.9 %copy-start.4 = (f32[8,128]{1,0:T(8,128)S(1)}, f32[8,128]{1,0:T(8,128)}, u32[]{:S(2)}) copy-start(f32[8,128]{1,0:T(8,128)} %get-tuple-element.36) | copy-start | bytes 12292

commit v4 on v3

--- a/solution.py
+++ b/solution.py
@@ -509,28 +509,34 @@
 
 
 def unpack(arrived_ref, tags_ref, slab_ref):
-    spot = iota((CL_DEV * MOST, 1), 0).astype(F32) + 1.0
-    parts = []
-    for g in range(GROUPS):
-        for half in range(2):
-            size = min((CAP if g < CHUNKS else OVER) - 128 * half, 128)
-            if size > 0:
-                parts.append(tags_ref[0, g, half : half + 1, :size])
-    row = jnp.concatenate(parts, axis=1)
-    onehot = jnp.where(spot == row, 1.0, 0.0).astype(BF16)
-    slab_ref[0] = jnp.dot(onehot, arrived_ref[0], preferred_element_type=F32).astype(BF16)
+    spot = iota((256, TOTAL), 0).astype(F32).astype(BF16)
+    for i in range(4):
+        parts = []
+        for g in range(GROUPS):
+            for half in range(2):
+                size = min((CAP if g < CHUNKS else OVER) - 128 * half, 128)
+                if size > 0:
+                    parts.append(tags_ref[i, g, half : half + 1, :size])
+        row = jnp.concatenate(parts, axis=1) - 1.0
+        for t in range(CL_DEV * MOST // 256):
+            line = jnp.broadcast_to(row - 256.0 * t, (16, TOTAL)).astype(BF16)
+            line = jnp.concatenate([line] * 16, axis=0)
+            onehot = jnp.where(spot == line, jnp.ones_like(line), jnp.zeros_like(line))
+            slab_ref[i, t * 256 : (t + 1) * 256, :] = jnp.dot(
+                onehot, arrived_ref[i], preferred_element_type=F32
+            ).astype(BF16)
 
 
 def run_unpack(arrived, tags):
     return pl.pallas_call(
         unpack,
-        grid=(WIDE,),
+        grid=(WIDE // 4,),
         out_shape=jax.ShapeDtypeStruct((WIDE, CL_DEV * MOST, PIECE), BF16),
         in_specs=[
-            pl.BlockSpec((1, TOTAL, PIECE), lambda b: (b, 0, 0)),
-            pl.BlockSpec((1, GROUPS, 2, 128), lambda b: (b, 0, 0, 0)),
+            pl.BlockSpec((4, TOTAL, PIECE), lambda b: (b, 0, 0)),
+            pl.BlockSpec((4, GROUPS, 2, 128), lambda b: (b, 0, 0, 0)),
         ],
-        out_specs=pl.BlockSpec((1, CL_DEV * MOST, PIECE), lambda b: (b, 0, 0)),
+        out_specs=pl.BlockSpec((4, CL_DEV * MOST, PIECE), lambda b: (b, 0, 0)),
         compiler_params=pltpu.CompilerParams(vmem_limit_bytes=32 * 2**20),
         name="unpack",
     )(arrived, tags)

time: 89.1 us -> 83.8 us (0.941)
  Pallas kernels: 84.6 us -> 79.5 us
    pallas_call x1, Pallas kernels: 14.7 us -> 9.61 us  [run_unpack(): pl.pallas_call(unpack, grid=(WIDE // 4,), out_shape=jax.ShapeDtypeStruct(...]
where the time goes in v4:
time: 83.8 us; the launch traced here: 83.6 us
  Pallas kernels  79.5 us (95%)
  other arithmetic  1.89 us (2%)
  between operations  1.34 us (2%)
    pallas_call x1, Pallas kernels, run_exchange(): pl.pallas_call(exchange, out_shape=(jax.ShapeDtypeStruct((WIDE, TOTAL, PI...  69.9 us
    pallas_call x1, Pallas kernels, run_unpack(): pl.pallas_call(unpack, grid=(WIDE // 4,), out_shape=jax.ShapeDtypeStruct(...  9.61 us

profile of v4, /device:TPU:1, one launch (start us, length us, event | category | flops | bytes accessed | tf_op | source)
XLA Modules:
  0.0 83.6 jit_solution(9580182876609492704)
XLA Ops:
  0.6 1.3 %pad_convert_fusion.query_ref = f32[8,128]{1,0:T(8,128)} fusion(bf16[4,128]{1,0:T(4,128)(2,1)} %param.17), kind=kLoop, calls=%fused_computation.46 | loop fusion | flops 1024 | bytes 5120 | tf_op jit(solution)/shard_map/jit(_pad)/pad | solution.py:614
  1.9 0.0 copy-start
  1.9 0.0 copy-start.1
  1.9 0.0 copy-start.2
  1.9 0.0 copy-start.3
  1.9 69.9 %exchange.1 = (bf16[16,752,128]{2,1,0:T(8,128)(2,1)}, f32[16,5,2,128]{3,2,1,0:T(2,128)S(1)}, f32[8,128]{1,0:T(8,128)}) custom-call(bf16[1024,1024]{1,0:T(8,128)(2,1)} %feats_hbm.1, bf16[1024,1024]{1,0:T(8,128)(2,1)} %w1_hbm.1, bf16[1024,1024]{1,0:T(8,128)(2,1)} %w2_hbm.1, bf16[1024,1024]{1,0:T(8,128)(2,1)} %w3_hbm.1, f32[1,1024]{1,0:T(1,128)} %bitcast.42, ...), custom_call_target="tpu_custom_call" | custom-call | tf_op jit(solution)/shard_map/exchange/pallas_call | solution.py:457
  71.8 0.6 slice_reduce_fusion
  73.1 0.0 copy-done
  73.1 0.0 copy-done.1
  73.1 0.0 copy-done.2
  73.1 0.0 copy-done.3
  73.1 0.0 copy-start.4
  73.1 9.9 %conditional.1 = (bf16[16,32,32,128]{3,2,1,0:T(8,128)(2,1)}) conditional(s32[]{:T(128)} %convert_element_type.39, (s32[1024,1]{0,1:T(1,128)S(1)}, s32[512]{0:T(512)S(1)}, bf16[1024,1024]{1,0:T(8,128)(2,1)S(1)}, bf16[1024,1024]{1,0:T(8,128)(2,1)}, bf16[1024,1024]{1,0:T(8,128)(2,1)}, /*index=5*/bf16[1024,1024]{1,0:T(8,128)(2,1)}, ...), branch_computations={%region_1.5_spmd, %region_5.6_spmd} | conditional | flops 8673079296 | bytes 102107448 | solution.py:619
  73.4 9.6 %unpack.1 = bf16[16,1024,128]{2,1,0:T(8,128)(2,1)} custom-call(bf16[16,752,128]{2,1,0:T(8,128)(2,1)} %get-tuple-element.29.arrived_ref, f32[16,5,2,128]{3,2,1,0:T(2,128)S(1)} %get-tuple-element.30.tags_ref), custom_call_target="tpu_custom_call" | custom-call | tf_op jit(solution)/shard_map/cond/branch_1_fun/unpack/pallas_call | solution.py:531
  83.0 0.0 copy-done.4
  83.0 0.6 copy.20
Async XLA Ops:
  1.9 71.2 %copy-start = (bf16[1024,1024]{1,0:T(8,128)(2,1)S(1)}, bf16[1024,1024]{1,0:T(8,128)(2,1)}, u32[]{:S(2)}) copy-start(bf16[1024,1024]{1,0:T(8,128)(2,1)} %feats_hbm.1) | copy-start | bytes 6291460
  1.9 71.2 %copy-start.1 = (f32[1024]{0:T(1024)S(1)}, f32[1024]{0:T(1024)}, u32[]{:S(2)}) copy-start(f32[1024]{0:T(1024)} %param.16) | copy-start | bytes 12292
  1.9 71.2 %copy-start.2 = (s32[1024,1]{0,1:T(1,128)S(1)}, s32[1024,1]{0,1:T(1,128)}, u32[]{:S(2)}) copy-start(s32[1024,1]{0,1:T(1,128)} %param.11) | copy-start | bytes 12292
  1.9 71.2 %copy-start.3 = (s32[512]{0:T(512)S(1)}, s32[512]{0:T(512)}, u32[]{:S(2)}) copy-start(s32[512]{0:T(512)} %param.12) | copy-start | bytes 6148
  73.1 9.9 %copy-start.4 = (f32[8,128]{1,0:T(8,128)S(1)}, f32[8,128]{1,0:T(8,128)}, u32[]{:S(2)}) copy-start(f32[8,128]{1,0:T(8,128)} %get-tuple-element.36) | copy-start | bytes 12292
